TPU v7x, 32 devices: a whole 2x2x4 slice. The times are simulated.
32 devices in a mesh: geo: 4 (over x, core), curve: 8 (over z, y).
Axes of the slice: x: 2, y: 2, z: 4, core: 2. Of those that a mesh axis runs over, the one named last changes fastest.
Arguments:
- tokens: bfloat16 [32768, 512], P(('geo', 'curve')), parts along dimension 0, may hold values from -80 to 80
- w_query: bfloat16 [512, 512], replicated, may hold values from -0.25 to 0.25
- w_keyval: bfloat16 [512, 1024], replicated, may hold values from -0.25 to 0.25
- w_out: bfloat16 [512, 512], replicated, may hold values from -0.25 to 0.25
- block_list: int32 [256, 12], P(('geo', 'curve')), parts along dimension 0, may hold values from 0 to 63, as said below
- block_count: int32 [256], P(('geo', 'curve')), parts along dimension 0, may hold values from 2 to 12, as said below
- bnd_ids: int32 [2048], P('geo'), parts along dimension 0, may hold values from 0 to 8191, as said below
Outputs:
- mixed: bfloat16 [32768, 512], P(('geo', 'curve')), parts along dimension 0
There are 4 independent parts, one for each index of `geo`. A program takes and returns all parts, laid end to end along the dimension named above; an argument that names none is the same for every part. Nothing has to cross between parts.
Inputs may be any that keep to these rules, and one draw needn't show every extreme that they name: `block_list`: entry 0 of row b is b itself; the other entries of a row are distinct blocks other than b whose owners lie at most two devices of curve away from b's owner (device index = block // 8); entries at or past block_count[b] are not used. `block_count`: it equals 12 on the first block of every device. `bnd_ids`: Distinct; listed in increasing order of owner id // 1024; exactly eight owners hold 128, 128, 96, 64, 48, 24, 16 and 8 of them, the other devices none.
All inputs are finite; a program needn't handle non-finite values.
Results may differ from a plain program's by a relative error of at most 0.012.
The roundings to bfloat16 on the way count: a program that leaves them out, or rounds other values in their place, can miss the bound.
Values may be sent and summed in bfloat16 or wider, within the bound.
A program may use at most 128 MiB of HBM per device.

v0:
```python
import functools

import jax
import jax.numpy as jnp
from jax import lax
from jax.experimental import pallas as pl
from jax.experimental.pallas import tpu as pltpu
from jax.sharding import PartitionSpec as P

HEADS = 8
BLOCK = 128
NB = 12
BCAP = 128
LOW = -1e30
ROWS = 256

FIRST, BOUND, MIDDLE, LAST = range(4)


def cast_dot(a, b, dims):
    out = lax.dot_general(a, b, (dims, ((), ())), preferred_element_type=jnp.float32)
    return out.astype(jnp.bfloat16)


def project(tok, wk, wvt, k_ref, vt_ref, norm_ref, base):
    width = wk.shape[0]
    feature = lax.broadcasted_iota(jnp.int32, (width, BLOCK), 0)
    head = lax.broadcasted_iota(jnp.int32, (width, BLOCK), 1)
    ind = jnp.where(feature >> 6 == head, 1.0, 0.0).astype(jnp.bfloat16)

    @pl.loop(0, tok.shape[0] // ROWS)
    def _(t):
        rows = tok[pl.ds(pl.multiple_of(t * ROWS, ROWS), ROWS), :]
        k = cast_dot(rows, wk[...], ((1,), (0,)))
        vt = cast_dot(wvt[...], rows, ((1,), (1,)))
        for i in range(ROWS // BLOCK):
            at = base + t * (ROWS // BLOCK) + i
            k_ref[at] = k[i * BLOCK:(i + 1) * BLOCK, :]
            vt_ref[at] = vt[:, i * BLOCK:(i + 1) * BLOCK]
        norm = jnp.dot(k * k, ind, preferred_element_type=jnp.float32)
        norm_ref[...] = jnp.maximum(norm_ref[...], jnp.max(norm, axis=0, keepdims=True))


def local_source(kind, slot, me):
    near = 3 - 2 * lax.rem(me, 2)
    if kind == FIRST:
        return jnp.where(slot == 2, 0, -1)
    if kind == MIDDLE:
        return jnp.where(slot == 0, 0, jnp.where(slot == 4, 1, jnp.where(slot == near, 2, -1)))
    return jnp.where(slot == 4 - near, 0, -1)


def make_plans(me, nqb, nbound, lists, counts, plan, plan_qb, plan_n):
    for kind in (FIRST, MIDDLE, LAST):
        def row(qb, at):
            def entry(i, n):
                rel = jnp.clip(lists[qb, i] - (me - 2) * nqb, 0, 5 * nqb - 1)
                slot = lax.div(rel, nqb)
                src = local_source(kind, slot, me)
                take = jnp.logical_and(i < counts[qb], src >= 0)
                plan[kind, n] = jnp.where(take, src * nqb + rel - slot * nqb, -1)
                return n + take.astype(jnp.int32)

            n = lax.fori_loop(0, NB, entry, at)
            plan[kind, n] = -1
            top = at + 2 * lax.div(n - at + 1, 2)

            @pl.loop(lax.div(at, 2), lax.div(top, 2))
            def _(j):
                plan_qb[kind, j] = qb
            return top

        top = lax.fori_loop(0, nqb, row, jnp.int32(0))
        plan[kind, top] = -1
        plan[kind, top + 1] = -1
        plan_qb[kind, lax.div(top, 2)] = 0
        plan_n[kind] = lax.div(top + 2, 4)
    each = nbound // BLOCK // 2

    @pl.loop(0, nqb * each)
    def _(j):
        plan[BOUND, 2 * j] = 2 * lax.rem(j, each)
        plan[BOUND, 2 * j + 1] = 2 * lax.rem(j, each) + 1
        plan_qb[BOUND, j] = lax.div(j, each)
    plan_n[BOUND] = nqb * each // 2


def phase(kind, nsrc, nbound, *refs):
    refs = list(refs)
    take = lambda n: [refs.pop(0) for _ in range(n)]
    toks = take(nsrc)
    wk, wvt = take(2)
    if kind == FIRST:
        me_ref, lists, counts, wqt = take(4)
    else:
        plan, plan_qb, plan_n, fast_in, qn_in, qbd, acc_in, m_in, l_in = take(9)
    if kind == LAST:
        wo, out = take(2)
    else:
        if kind == FIRST:
            plan, plan_qb, plan_n, qn_out, qbd = take(5)
        (fast_out,) = take(1)
    acc, m_ref, l_ref, k_ref, vt_ref, p_ref, norm_ref = take(7)
    nqb, pairs = qbd.shape[0], qbd.shape[1]

    norm_ref[...] = jnp.zeros_like(norm_ref)
    if kind == FIRST:
        (qn_ref,) = take(1)
        make_plans(me_ref[0], nqb, nbound, lists, counts, plan, plan_qb, plan_n)
        qn_ref[...] = jnp.zeros_like(qn_ref)
        zero = jnp.zeros((64, BLOCK), jnp.bfloat16)

        @pl.loop(0, toks[0].shape[0] // ROWS)
        def _(t):
            rows = toks[0][pl.ds(pl.multiple_of(t * ROWS, ROWS), ROWS), :]
            q = lax.dot_general(wqt[...], rows, (((1,), (1,)), ((), ())), preferred_element_type=jnp.float32)
            q = q.astype(jnp.bfloat16) * jnp.bfloat16(0.125)
            for i in range(ROWS // BLOCK):
                for hp in range(pairs):
                    cut = q[hp * BLOCK:(hp + 1) * BLOCK, i * BLOCK:(i + 1) * BLOCK]
                    at = t * (ROWS // BLOCK) + i
                    qbd[at, hp, :64, :] = jnp.concatenate([cut[:64], zero], axis=1)
                    qbd[at, hp, 64:, :] = jnp.concatenate([zero, cut[64:]], axis=1)
            q = q.astype(jnp.float32)
            for h in range(2 * pairs):
                part = q[h * 64:(h + 1) * 64, :]
                qn_ref[...] = jnp.maximum(qn_ref[...], jnp.sum(part * part, axis=0, keepdims=True))

        acc[...] = jnp.zeros_like(acc)
        l_ref[...] = jnp.zeros_like(l_ref)
        qn = jnp.max(qn_ref[...])
        qn_out[0] = qn
    else:
        acc[...] = acc_in[...]
        l_ref[...] = l_in[...]
        m_ref[...] = m_in[...]
        qn = qn_in[0]

    for s, tok in enumerate(toks):
        project(tok, wk, wvt, k_ref, vt_ref, norm_ref, s * (tok.shape[0] // BLOCK))
    small = qn * jnp.max(norm_ref[...]) <= 3600.0
    fast = small if kind == FIRST else jnp.logical_and(small, fast_in[0] == 1)
    if kind == FIRST:
        m_ref[...] = jnp.full_like(m_ref, jnp.where(fast, 0.0, LOW))
    if kind != LAST:
        fast_out[0] = fast.astype(jnp.int32)
    count = plan_n[kind]

    def blocks(item):
        return jnp.maximum(plan[kind, 2 * item], 0), jnp.maximum(plan[kind, 2 * item + 1], 0)

    def scores(item):
        b0, b1 = blocks(item)
        bias0 = jnp.where(plan[kind, 2 * item] < 0, LOW, 0.0).astype(jnp.float32)
        bias1 = jnp.where(plan[kind, 2 * item + 1] < 0, LOW, 0.0).astype(jnp.float32)
        qb = plan_qb[kind, item]
        made = []
        for hp in range(pairs):
            cut = slice(hp * BLOCK, (hp + 1) * BLOCK)
            k = jnp.concatenate([k_ref[b0, :, cut], k_ref[b1, :, cut]], axis=0)
            s = jnp.dot(k, qbd[qb, hp], preferred_element_type=jnp.float32)
            made.append((s[:BLOCK] + bias0, s[BLOCK:] + bias1))
        return made

    def values(item, hp):
        b0, b1 = blocks(item)
        cut = slice(hp * BLOCK, (hp + 1) * BLOCK)
        v = jnp.concatenate([vt_ref[b0, cut, :], vt_ref[b1, cut, :]], axis=1)
        return jnp.concatenate([v, jnp.ones((16, 2 * BLOCK), jnp.bfloat16)], axis=0)

    @pl.when(fast)
    def _():
        def weigh(item, slot):
            for hp, halves in enumerate(scores(item)):
                for i, s in enumerate(halves):
                    p_ref[slot, hp, i * BLOCK:(i + 1) * BLOCK, :] = jnp.exp(s).astype(jnp.bfloat16)

        def gather(item, slot):
            qb = plan_qb[kind, item]
            pvs = [
                jnp.dot(values(item, hp), p_ref[slot, hp], preferred_element_type=jnp.float32)
                for hp in range(pairs)
            ]
            for hp, pv in enumerate(pvs):
                row = qb * pairs + hp
                acc[row, :64, :] = acc[row, :64, :] + pv[:64, :BLOCK]
                acc[row, 64:, :] = acc[row, 64:, :] + pv[64:BLOCK, BLOCK:]
                l_ref[row] = l_ref[row] + pv[BLOCK:BLOCK + 1, :]

        p_ref[1] = jnp.zeros_like(p_ref[1])

        def two(t, carry):
            gather(jnp.maximum(2 * t - 1, 0), 1)
            weigh(2 * t, 0)
            gather(2 * t, 0)
            weigh(2 * t + 1, 1)
            return carry

        lax.fori_loop(0, count, two, 0)
        gather(jnp.maximum(2 * count - 1, 0), 1)

    @pl.when(jnp.logical_not(fast))
    def _():
        def one(item, carry):
            qb = plan_qb[kind, item]
            for hp, halves in enumerate(scores(item)):
                row = qb * pairs + hp
                s = jnp.concatenate(halves, axis=0)
                m_old = m_ref[row]
                m_new = jnp.maximum(m_old, jnp.max(s, axis=0, keepdims=True))
                p = jnp.exp(s - m_new).astype(jnp.bfloat16)
                alpha = jnp.exp(m_old - m_new)
                pv = jnp.dot(values(item, hp), p, preferred_element_type=jnp.float32)
                acc[row, :64, :] = acc[row, :64, :] * alpha[:, :BLOCK] + pv[:64, :BLOCK]
                acc[row, 64:, :] = acc[row, 64:, :] * alpha[:, BLOCK:] + pv[64:BLOCK, BLOCK:]
                l_ref[row] = l_ref[row] * alpha + pv[BLOCK:BLOCK + 1, :]
                m_ref[row] = m_new
            return carry

        lax.fori_loop(0, 2 * count, one, 0)

    if kind == LAST:
        @pl.loop(0, nqb)
        def _(qb):
            parts = []
            for hp in range(pairs):
                row = qb * pairs + hp
                inv = 1.0 / l_ref[row]
                parts.append(acc[row, :64, :] * inv[:, :BLOCK])
                parts.append(acc[row, 64:, :] * inv[:, BLOCK:])
            ctx = jnp.concatenate(parts, axis=0).T.astype(jnp.bfloat16)
            out[pl.ds(pl.multiple_of(qb * BLOCK, BLOCK), BLOCK), :] = cast_dot(ctx, wo[...], ((1,), (0,)))


def run_phase(kind, toks, wk, wvt, nbound, lists=None, wqt=None, state=None, wo=None):
    width = wk.shape[0]
    pairs = width // BLOCK
    nkb = sum(t.shape[0] for t in toks) // BLOCK
    vmem, smem = pl.BlockSpec(memory_space=pltpu.VMEM), pl.BlockSpec(memory_space=pltpu.SMEM)
    args, specs = list(toks) + [wk, wvt], [vmem] * (len(toks) + 2)
    if kind == FIRST:
        args += list(lists) + [wqt]
        specs += [smem] * 3 + [vmem]
        nqb = toks[0].shape[0] // BLOCK
    else:
        args += list(state)
        specs += [smem] * 5 + [vmem] * 4
        nqb = state[5].shape[0]
    if kind == LAST:
        args.append(wo)
        specs.append(vmem)
    sums = [(nqb * pairs, BLOCK, BLOCK), (nqb * pairs, 1, 2 * BLOCK), (nqb * pairs, 1, 2 * BLOCK)]
    outs, out_specs, scratch = [], [], []
    if kind == LAST:
        outs.append(jax.ShapeDtypeStruct((nqb * BLOCK, width), jnp.bfloat16))
        out_specs.append(vmem)
        scratch += [pltpu.VMEM(s, jnp.float32) for s in sums]
    else:
        if kind == FIRST:
            room = nqb * NB + 16
            outs += [
                jax.ShapeDtypeStruct((4, room), jnp.int32),
                jax.ShapeDtypeStruct((4, room), jnp.int32),
                jax.ShapeDtypeStruct((4,), jnp.int32),
                jax.ShapeDtypeStruct((1,), jnp.float32),
                jax.ShapeDtypeStruct((nqb, pairs, BLOCK, 2 * BLOCK), jnp.bfloat16),
            ]
            out_specs += [smem] * 4 + [vmem]
        outs.append(jax.ShapeDtypeStruct((1,), jnp.int32))
        out_specs.append(smem)
        outs += [jax.ShapeDtypeStruct(s, jnp.float32) for s in sums]
        out_specs += [vmem] * 3
    scratch += [
        pltpu.VMEM((nkb, BLOCK, width), jnp.bfloat16),
        pltpu.VMEM((nkb, width, BLOCK), jnp.bfloat16),
        pltpu.VMEM((2, pairs, 2 * BLOCK, 2 * BLOCK), jnp.bfloat16),
        pltpu.VMEM((1, BLOCK), jnp.float32),
    ]
    if kind == FIRST:
        scratch.append(pltpu.VMEM((1, ROWS), jnp.float32))
    units = {FIRST: 18, BOUND: 32, MIDDLE: 34, LAST: 11}[kind]
    cost = pl.CostEstimate(
        flops=units * 8 * 2 * BLOCK ** 3 * 8 + nkb * BLOCK * width * width * 4,
        bytes_accessed=8 << 20,
        transcendentals=units * 8 * BLOCK * BLOCK,
    )
    return pl.pallas_call(
        functools.partial(phase, kind, len(toks), nbound),
        out_shape=outs,
        in_specs=specs,
        out_specs=out_specs,
        scratch_shapes=scratch,
        compiler_params=pltpu.CompilerParams(vmem_limit_bytes=40 << 20),
        cost_estimate=cost,
        name=("attend_own", "attend_bound", "attend_middle", "attend_last")[kind],
    )(*args)


def send(value, pairs):
    return lax.ppermute(value, "curve", pairs)


def on_device(tokens, w_query, w_keyval, w_out, block_list, block_count, bnd_ids):
    tok_dev, width = tokens.shape
    nbound = bnd_ids.shape[0]
    size = lax.axis_size("curve")
    member = lax.axis_index("curve")
    everyone = range(size)

    owner = bnd_ids // tok_dev
    slots = jnp.arange(BCAP, dtype=jnp.int32)
    my_start = jnp.sum((owner < member).astype(jnp.int32))
    padded_ids = jnp.concatenate([bnd_ids, jnp.zeros((BCAP,), jnp.int32)])
    my_ids = lax.dynamic_slice_in_dim(padded_ids, my_start, BCAP) - member * tok_dev
    pick = (my_ids[:, None] == jnp.arange(tok_dev, dtype=jnp.int32)[None, :]).astype(jnp.bfloat16)
    rows = jnp.dot(pick, tokens, preferred_element_type=jnp.float32).astype(jnp.bfloat16)
    gathered = lax.all_gather(rows, "curve", axis=0, tiled=True)

    from_two_behind = send(tokens, [(i, i + 2) for i in everyone if i + 2 < size])
    from_two_ahead = send(tokens, [(i, i - 2) for i in everyone if i >= 2])
    mate = send(tokens, [(i, i ^ 1) for i in everyone])

    wk = w_keyval[:, :width]
    wvt = w_keyval[:, width:].T
    lists = (member.reshape(1).astype(jnp.int32), block_list, block_count)
    *plan, qn, qbd, fast, acc, top, total = run_phase(
        FIRST, [tokens], wk, wvt, nbound, lists=lists, wqt=w_query.T
    )

    slot_range = jnp.arange(nbound, dtype=jnp.int32)
    owner_start = jnp.sum((owner[None, :] < owner[:, None]).astype(jnp.int32), axis=1)
    source = owner * BCAP + slot_range - owner_start
    choose = (source[:, None] == jnp.arange(size * BCAP, dtype=jnp.int32)[None, :]).astype(jnp.bfloat16)
    bound = jnp.dot(choose, gathered, preferred_element_type=jnp.float32).astype(jnp.bfloat16)
    fast, acc, top, total = run_phase(
        BOUND, [bound], wk, wvt, nbound, state=[*plan, fast, qn, qbd, acc, top, total]
    )

    after = jnp.minimum(fast[0], 0)
    half = tok_dev // 2
    relay = jnp.where(member % 2 == after, from_two_ahead[:half], from_two_behind[:half])
    low = send(relay, [(i, i ^ 1) for i in everyone])
    hops = [(i, i + 2 - 4 * (i % 2)) for i in everyone]
    upper = lax.dynamic_slice_in_dim(mate, half + after, half)
    high = send(upper, [(a, b) for a, b in hops if 0 <= b < size])

    fast, acc, top, total = run_phase(
        MIDDLE,
        [from_two_behind, from_two_ahead, mate],
        wk,
        wvt,
        nbound,
        state=[*plan, fast, qn, qbd, acc, top, total],
    )
    far = jnp.concatenate([low, high], axis=0)
    (mixed,) = run_phase(
        LAST, [far], wk, wvt, nbound, state=[*plan, fast, qn, qbd, acc, top, total], wo=w_out
    )
    return mixed


def solution(mesh):
    in_specs = (
        P(("geo", "curve"), None),
        P(),
        P(),
        P(),
        P(("geo", "curve"), None),
        P(("geo", "curve")),
        P("geo"),
    )
    out_specs = P(("geo", "curve"), None)
    return jax.shard_map(
        on_device, mesh=mesh, in_specs=in_specs, out_specs=out_specs, check_vma=False
    )
```

profile of v0, /device:TPU:15, one launch (start us, length us, event | category | flops | bytes accessed | tf_op | source)
XLA Modules:
  0.0 129.9 jit_solution(4842461920975574235)
XLA Ops:
  6.5 0.0 all-gather.2.cloned.1.call-start
  6.5 1.3 %convert_reduce_fusion.1 = (s32[]{:T(128)}, s32[512]{0:T(512)S(1)}) fusion(s32[]{:T(128)} %axis_index.12, s32[512]{0:T(512)} %param.13), kind=kLoop, calls=%fused_computation.16 | loop fusion | flops 9215 | bytes 4104 | tf_op jit(solution)/shard_map/reduce_sum | solution.py:312
  9.8 0.8 fusion.6
  10.6 0.0 copy-start.11
  10.6 2.3 %convolution_convert_fusion = bf16[128,512]{1,0:T(8,128)(2,1)} fusion(bf16[1024,512]{1,0:T(8,128)(2,1)} %refs_0_.1, s32[128]{0:T(128)S(1)} %fusion.6), kind=kOutput, calls=%fused_computation.3 | convolution fusion | flops 134414336 | bytes 1180160 | tf_op jit(solution)/shard_map/dot_general | solution.py:316
  12.9 0.0 all-gather.2.cloned.1.call-update
  12.9 2.1 %collective-permute-start = (bf16[1024,512]{1,0:T(8,128)(2,1)}, bf16[1024,512]{1,0:T(8,128)(2,1)}, u32[]{:S(2)}, u32[]{:S(2)}) collective-permute-start(bf16[1024,512]{1,0:T(8,128)(2,1)} %refs_0_.1), channel_id=1, source_target_pairs={{2,0},{3,1},{4,2},{5,3},{6,4},{7,5},{10,8},{11,9},{12,10},{13,11},... | collective-permute-start | bytes 3145736 | tf_op jit(solution)/shard_map/ppermute | solution.py:300
  15.0 3.2 %collective-permute-start.1 = (bf16[1024,512]{1,0:T(8,128)(2,1)}, bf16[1024,512]{1,0:T(8,128)(2,1)}, u32[]{:S(2)}, u32[]{:S(2)}) collective-permute-start(bf16[1024,512]{1,0:T(8,128)(2,1)} %refs_0_.1), channel_id=1, source_target_pairs={{0,2},{1,3},{2,4},{3,5},{4,6},{5,7},{8,10},{9,11},{10,12},{11,13},... | collective-permute-start | bytes 3145736 | tf_op jit(solution)/shard_map/ppermute | solution.py:300
  18.2 0.3 collective-permute-start.3
  18.5 0.0 copy-start
  18.5 0.0 copy-start.2
  18.5 0.0 copy-start.3
  18.5 1.4 %fusion.7 = (bf16[512,512]{1,0:T(8,128)(2,1)S(1)}, bf16[512,512]{1,0:T(8,128)(2,1)S(1)}) fusion(bf16[512,1024]{1,0:T(8,128)(2,1)} %param.9), kind=kLoop, calls=%fused_computation.22 | loop fusion | bytes 2097152 | tf_op jit(solution)/shard_map/slice | solution.py:324
  19.9 0.2 copy.12
  20.1 0.0 copy-done.11
  20.1 0.2 copy.11
  20.3 0.2 convert_reduce_fusion
  20.6 0.0 copy-done
  20.6 0.0 copy-done.2
  20.6 0.0 copy-done.3
  20.6 18.2 %attend_own.1 = (s32[4,112]{1,0:T(4,128)S(1)}, s32[4,112]{1,0:T(4,128)S(1)}, s32[4]{0:T(128)S(1)}, f32[1]{0:T(128)}, bf16[8,4,128,256]{3,2,1,0:T(8,128)(2,1)S(1)...) custom-call(bf16[1024,512]{1,0:T(8,128)(2,1)S(1)} %copy-done, ...), custom_call_target="tpu_custom_call" | custom-call | flops 5905580032 | bytes 8388608 | tf_op jit(solution)/shard_map/attend_own/pallas_call | solution.py:287
  38.8 0.0 copy-start.4
  38.8 1.3 %copy-done.4 = bf16[8,4,128,256]{3,2,1,0:T(8,128)(2,1)} copy-done((bf16[8,4,128,256]{3,2,1,0:T(8,128)(2,1)}, bf16[8,4,128,256]{3,2,1,0:T(8,128)(2,1)S(1)}, u32[]{:S(2)}) %copy-start.4) | copy-done | bytes 2097176
  40.1 0.0 copy-start.7
  40.1 1.3 %copy-done.7 = f32[32,128,128]{2,1,0:T(8,128)} copy-done((f32[32,128,128]{2,1,0:T(8,128)}, f32[32,128,128]{2,1,0:T(8,128)S(1)}, u32[]{:S(2)}) %copy-start.7) | copy-done | bytes 2097176
  41.5 15.1 %all-gather.2.cloned.1.call-done = bf16[1024,512]{1,0:T(8,128)(2,1)} async-done(((bf16[128,512]{1,0:T(8,128)(2,1)}), bf16[1024,512]{1,0:T(8,128)(2,1)}) %all-gather.2.cloned.1.call-update) | async-done | bytes 1048592 | tf_op jit(solution)/shard_map/all_gather | solution.py:317
  56.6 0.0 copy-start.5
  56.6 2.1 %fusion.1.refs_0_ = bf16[512,512]{1,0:T(8,128)(2,1)S(1)} fusion(bf16[1024,512]{1,0:T(8,128)(2,1)} %all-gather.2.cloned.1.call-done, s32[512]{0:T(512)S(1)} %add_subtract_fusion), kind=kOutput, calls=%fused_computation.2 | convolution fusion | flops 537657344 | bytes 1574912 | tf_op jit(solution)/shard_map/dot_general | solution.py:334
  58.7 0.0 copy-done.5
  58.7 0.0 copy-start.8
  58.7 1.6 %copy-done.8 = f32[32,128,128]{2,1,0:T(8,128)S(1)} copy-done((f32[32,128,128]{2,1,0:T(8,128)S(1)}, f32[32,128,128]{2,1,0:T(8,128)}, u32[]{:S(2)}) %copy-start.8) | copy-done | bytes 2097176
  60.3 13.7 %attend_bound.1 = (s32[1]{0:T(128)}, f32[32,128,128]{2,1,0:T(8,128)S(1)}, f32[32,1,256]{2,1,0:T(1,128)S(1)}, f32[32,1,256]{2,1,0:T(1,128)S(1)}) custom-call(bf16[512,512]{1,0:T(8,128)(2,1)S(1)} %fusion.1.refs_0_, bf16[512,512]{1,0:T(8,128)(2,1)S(1)} %get-tuple-element.42.refs_1_.refs_3_, bf16[512,512]{1,0:T(8,128)(2,1)S(1)} %bitcast.7, ...), custom_call_target="tpu_custom_call" | custom-call | flops 9126805504 | bytes 8388608 | tf_op jit(solution)/shard_map/attend_bound/pallas_call | solution.py:287
  74.0 0.0 copy-start.9
  74.0 1.3 %copy-done.9 = f32[32,128,128]{2,1,0:T(8,128)} copy-done((f32[32,128,128]{2,1,0:T(8,128)}, f32[32,128,128]{2,1,0:T(8,128)S(1)}, u32[]{:S(2)}) %copy-start.9) | copy-done | bytes 2097176
  76.0 0.0 collective-permute-done.refs_1_
  76.0 0.0 collective-permute-done.1.refs_0_
  76.0 1.3 slice_select_fusion
  77.3 0.4 collective-permute-start.2
  77.6 0.0 collective-permute-done.3.refs_2_
  77.7 1.2 constant_dynamic-slice_fusion
  78.8 3.5 %collective-permute-start.4 = (bf16[512,512]{1,0:T(8,128)(2,1)S(1)}, bf16[512,512]{1,0:T(8,128)(2,1)S(1)}, u32[]{:S(2)}, u32[]{:S(2)}) collective-permute-start(bf16[512,512]{1,0:T(8,128)(2,1)S(1)} %constant_dynamic-slice_fusion), channel_id=1, source_target_pairs={{0,2},{2,4},{3,1},{4,6},{5,3},{7,5},{8,10},{10,12},{11,9},{12,14},... | collective-permute-start | bytes 1572872 | tf_op jit(solution)/shard_map/ppermute | solution.py:300
  82.3 0.0 copy-start.6
  82.3 1.6 %copy-done.6 = bf16[8,4,128,256]{3,2,1,0:T(8,128)(2,1)S(1)} copy-done((bf16[8,4,128,256]{3,2,1,0:T(8,128)(2,1)S(1)}, bf16[8,4,128,256]{3,2,1,0:T(8,128)(2,1)}, u32[]{:S(2)}) %copy-start.6) | copy-done | bytes 2097176
  83.9 0.0 copy-start.10
  83.9 1.6 %copy-done.10 = f32[32,128,128]{2,1,0:T(8,128)S(1)} copy-done((f32[32,128,128]{2,1,0:T(8,128)S(1)}, f32[32,128,128]{2,1,0:T(8,128)}, u32[]{:S(2)}) %copy-start.10) | copy-done | bytes 2097176
  85.5 24.0 %attend_middle.1 = (s32[1]{0:T(128)}, f32[32,128,128]{2,1,0:T(8,128)S(1)}, f32[32,1,256]{2,1,0:T(1,128)S(1)}, f32[32,1,256]{2,1,0:T(1,128)S(1)}) custom-call(bf16[1024,512]{1,0:T(8,128)(2,1)} %collective-permute-done.1.refs_0_, bf16[1024,512]{1,0:T(8,128)(2,1)} %collective-permute-done.refs_1_, bf16[1024,512]{1,0:T(8,128)(2,1)} %collective-permute-done.3.refs_2_, ...), custom_call_target="tpu_custom_call" | custom-call | flops 12348030976 | bytes 8388608 | tf_op jit(solution)/shard_map/attend_middle/pallas_call | solution.py:287
  109.6 0.0 copy-start.1
  109.6 0.0 collective-permute-done.2
  109.6 0.0 collective-permute-done.4
  109.6 0.1 pad_maximum_fusion.refs_0_
  109.7 0.9 copy-done.1
  110.6 12.5 %attend_last.1 = bf16[1024,512]{1,0:T(8,128)(2,1)} custom-call(bf16[1024,512]{1,0:T(8,128)(2,1)S(1)} %pad_maximum_fusion.refs_0_, bf16[512,512]{1,0:T(8,128)(2,1)S(1)} %get-tuple-element.42.refs_1_.refs_3_, bf16[512,512]{1,0:T(8,128)(2,1)S(1)} %bitcast.9, s32[4,112]{1,0:T(4,128)S(1)} %get-tuple-element.22.refs_3_.refs_5_, ...), custom_call_target="tpu_custom_call" | custom-call | flops 4026531840 | bytes 8388608 | tf_op jit(solution)/shard_map/attend_last/pallas_call | solution.py:287
  (1 shorter events, 0.0 us)
Async XLA Ops:
  6.5 50.0 %all-gather.2.cloned.1.call-start = ((), (), s32[]{:S(2)}) async-start(), calls=%async_computation | async-start | bytes 1179648 | tf_op jit(solution)/shard_map/all_gather | solution.py:317
  10.6 9.5 %copy-start.11 = (bf16[512,512]{1,0:T(8,128)(2,1)S(1)}, bf16[512,512]{1,0:T(8,128)(2,1)}, u32[]{:S(2)}) copy-start(bf16[512,512]{1,0:T(8,128)(2,1)} %param.8) | copy-start | bytes 1572868
  12.9 63.1 %collective-permute-start = (bf16[1024,512]{1,0:T(8,128)(2,1)}, bf16[1024,512]{1,0:T(8,128)(2,1)}, u32[]{:S(2)}, u32[]{:S(2)}) collective-permute-start(bf16[1024,512]{1,0:T(8,128)(2,1)} %refs_0_.1), channel_id=1, source_target_pairs={{2,0},{3,1},{4,2},{5,3},{6,4},{7,5},{10,8},{11,9},{12,10},{13,11},... | collective-permute-start | bytes 3145736 | tf_op jit(solution)/shard_map/ppermute | solution.py:300
  15.0 61.0 %collective-permute-start.1 = (bf16[1024,512]{1,0:T(8,128)(2,1)}, bf16[1024,512]{1,0:T(8,128)(2,1)}, u32[]{:S(2)}, u32[]{:S(2)}) collective-permute-start(bf16[1024,512]{1,0:T(8,128)(2,1)} %refs_0_.1), channel_id=1, source_target_pairs={{0,2},{1,3},{2,4},{3,5},{4,6},{5,7},{8,10},{9,11},{10,12},{11,13},... | collective-permute-start | bytes 3145736 | tf_op jit(solution)/shard_map/ppermute | solution.py:300
  18.2 59.5 %collective-permute-start.3 = (bf16[1024,512]{1,0:T(8,128)(2,1)}, bf16[1024,512]{1,0:T(8,128)(2,1)}, u32[]{:S(2)}, u32[]{:S(2)}) collective-permute-start(bf16[1024,512]{1,0:T(8,128)(2,1)} %refs_0_.1), channel_id=1, source_target_pairs={{0,1},{1,0},{2,3},{3,2},{4,5},{5,4},{6,7},{7,6},{8,9},{9,8},{10,11... | collective-permute-start | bytes 3145736 | tf_op jit(solution)/shard_map/ppermute | solution.py:300
  18.5 2.1 %copy-start = (bf16[1024,512]{1,0:T(8,128)(2,1)S(1)}, bf16[1024,512]{1,0:T(8,128)(2,1)}, u32[]{:S(2)}) copy-start(bf16[1024,512]{1,0:T(8,128)(2,1)} %refs_0_.1) | copy-start | bytes 3145732
  18.5 2.1 %copy-start.2 = (s32[8,12]{1,0:T(8,128)S(1)}, s32[8,12]{1,0:T(8,128)}, u32[]{:S(2)}) copy-start(s32[8,12]{1,0:T(8,128)} %refs_4_.1) | copy-start | bytes 1156
  18.5 2.1 %copy-start.3 = (s32[8]{0:T(128)S(1)}, s32[8]{0:T(128)}, u32[]{:S(2)}) copy-start(s32[8]{0:T(128)} %refs_5_.1) | copy-start | bytes 100
  38.8 1.3 %copy-start.4 = (bf16[8,4,128,256]{3,2,1,0:T(8,128)(2,1)}, bf16[8,4,128,256]{3,2,1,0:T(8,128)(2,1)S(1)}, u32[]{:S(2)}) copy-start(bf16[8,4,128,256]{3,2,1,0:T(8,128)(2,1)S(1)} %get-tuple-element.27.refs_8_.refs_10_) | copy-start | bytes 6291460
  40.1 1.3 %copy-start.7 = (f32[32,128,128]{2,1,0:T(8,128)}, f32[32,128,128]{2,1,0:T(8,128)S(1)}, u32[]{:S(2)}) copy-start(f32[32,128,128]{2,1,0:T(8,128)S(1)} %get-tuple-element.28.refs_9_) | copy-start | bytes 6291460
  56.6 2.1 %copy-start.5 = (bf16[8,4,128,256]{3,2,1,0:T(8,128)(2,1)S(1)}, bf16[8,4,128,256]{3,2,1,0:T(8,128)(2,1)}, u32[]{:S(2)}) copy-start(bf16[8,4,128,256]{3,2,1,0:T(8,128)(2,1)} %copy-done.4) | copy-start | bytes 6291460
  58.7 1.6 %copy-start.8 = (f32[32,128,128]{2,1,0:T(8,128)S(1)}, f32[32,128,128]{2,1,0:T(8,128)}, u32[]{:S(2)}) copy-start(f32[32,128,128]{2,1,0:T(8,128)} %copy-done.7) | copy-start | bytes 6291460
  74.0 1.3 %copy-start.9 = (f32[32,128,128]{2,1,0:T(8,128)}, f32[32,128,128]{2,1,0:T(8,128)S(1)}, u32[]{:S(2)}) copy-start(f32[32,128,128]{2,1,0:T(8,128)S(1)} %get-tuple-element.32.refs_11_) | copy-start | bytes 6291460
  77.3 32.3 %collective-permute-start.2 = (bf16[512,512]{1,0:T(8,128)(2,1)S(1)}, bf16[512,512]{1,0:T(8,128)(2,1)S(1)}, u32[]{:S(2)}, u32[]{:S(2)}) collective-permute-start(bf16[512,512]{1,0:T(8,128)(2,1)S(1)} %slice_select_fusion), channel_id=1, source_target_pairs={{0,1},{1,0},{2,3},{3,2},{4,5},{5,4},{6,7},{7,6},{8,9},{9,8},{10,11... | collective-permute-start | bytes 1572872 | tf_op jit(solution)/shard_map/ppermute | solution.py:300
  78.8 30.8 %collective-permute-start.4 = (bf16[512,512]{1,0:T(8,128)(2,1)S(1)}, bf16[512,512]{1,0:T(8,128)(2,1)S(1)}, u32[]{:S(2)}, u32[]{:S(2)}) collective-permute-start(bf16[512,512]{1,0:T(8,128)(2,1)S(1)} %constant_dynamic-slice_fusion), channel_id=1, source_target_pairs={{0,2},{2,4},{3,1},{4,6},{5,3},{7,5},{8,10},{10,12},{11,9},{12,14},... | collective-permute-start | bytes 1572872 | tf_op jit(solution)/shard_map/ppermute | solution.py:300
  82.3 1.6 %copy-start.6 = (bf16[8,4,128,256]{3,2,1,0:T(8,128)(2,1)S(1)}, bf16[8,4,128,256]{3,2,1,0:T(8,128)(2,1)}, u32[]{:S(2)}) copy-start(bf16[8,4,128,256]{3,2,1,0:T(8,128)(2,1)} %copy-done.4) | copy-start | bytes 6291460
  83.9 1.6 %copy-start.10 = (f32[32,128,128]{2,1,0:T(8,128)S(1)}, f32[32,128,128]{2,1,0:T(8,128)}, u32[]{:S(2)}) copy-start(f32[32,128,128]{2,1,0:T(8,128)} %copy-done.9) | copy-start | bytes 6291460
  109.6 1.0 copy-start.1
Sparse Core Ops, SparseCore 0:
  13.0 43.5 all-gather.1
where the time goes:
time: 132 us; the launch traced here: 130 us
  Pallas kernels  68.4 us (52%)
  between operations  16.2 us (12%)
  waiting for transfers between devices  15.1 us (11%)
  local copies, waits for them, and re-layouts  12.6 us (10%)
  starting transfers between devices  9.46 us (7%)
  matrix products  4.42 us (3%)
  other arithmetic  3.67 us (3%)
    pallas_call x4, Pallas kernels, run_phase(): pl.pallas_call(functools.partial(phase, kind, len(toks), nbound), out_sha...  68.4 us
    all_gather x1, waiting for transfers between devices, on_device(): gathered = lax.all_gather(rows, 'curve', axis=0, tiled=True)  15.1 us
    unnamed x26, local copies, waits for them, and re-layouts  10.1 us
    ppermute x5, starting transfers between devices, send(): return lax.ppermute(value, 'curve', pairs)  9.46 us
  transfers between devices with their start and end apart: 6, of which 1 were waited for; matrix products, arithmetic and copies ran while one was open for 5% of the time, Pallas kernels for 43%

commit v1 on v0

--- a/solution.py
+++ b/solution.py
@@ -14,7 +14,8 @@
 LOW = -1e30
 ROWS = 256
 
-FIRST, BOUND, MIDDLE, LAST = range(4)
+FIRST, MIDDLE, LAST = range(3)
+PLAN_LEN = 128
 
 
 def cast_dot(a, b, dims):
@@ -50,7 +51,7 @@
     return jnp.where(slot == 4 - near, 0, -1)
 
 
-def make_plans(me, nqb, nbound, lists, counts, plan, plan_qb, plan_n):
+def make_plans(me, nqb, nbound, lists, counts, plan):
     for kind in (FIRST, MIDDLE, LAST):
         def row(qb, at):
             def entry(i, n):
@@ -64,25 +65,21 @@
             n = lax.fori_loop(0, NB, entry, at)
             plan[kind, n] = -1
             top = at + 2 * lax.div(n - at + 1, 2)
+            if kind == LAST:
+                for j in range(nbound // BLOCK):
+                    plan[kind, top + j] = nqb + j
+                top = top + nbound // BLOCK
 
             @pl.loop(lax.div(at, 2), lax.div(top, 2))
             def _(j):
-                plan_qb[kind, j] = qb
+                plan[4 + kind, j] = qb
             return top
 
         top = lax.fori_loop(0, nqb, row, jnp.int32(0))
         plan[kind, top] = -1
         plan[kind, top + 1] = -1
-        plan_qb[kind, lax.div(top, 2)] = 0
-        plan_n[kind] = lax.div(top + 2, 4)
-    each = nbound // BLOCK // 2
-
-    @pl.loop(0, nqb * each)
-    def _(j):
-        plan[BOUND, 2 * j] = 2 * lax.rem(j, each)
-        plan[BOUND, 2 * j + 1] = 2 * lax.rem(j, each) + 1
-        plan_qb[BOUND, j] = lax.div(j, each)
-    plan_n[BOUND] = nqb * each // 2
+        plan[4 + kind, lax.div(top, 2)] = 0
+        plan[7, kind] = lax.div(top + 2, 4)
 
 
 def phase(kind, nsrc, nbound, *refs):
@@ -93,20 +90,18 @@
     if kind == FIRST:
         me_ref, lists, counts, wqt = take(4)
     else:
-        plan, plan_qb, plan_n, fast_in, qn_in, qbd, acc_in, m_in, l_in = take(9)
+        plan, qbd, acc_in, m_in, l_in = take(5)
     if kind == LAST:
         wo, out = take(2)
-    else:
-        if kind == FIRST:
-            plan, plan_qb, plan_n, qn_out, qbd = take(5)
-        (fast_out,) = take(1)
+    elif kind == FIRST:
+        plan, qbd = take(2)
     acc, m_ref, l_ref, k_ref, vt_ref, p_ref, norm_ref = take(7)
     nqb, pairs = qbd.shape[0], qbd.shape[1]
 
     norm_ref[...] = jnp.zeros_like(norm_ref)
     if kind == FIRST:
         (qn_ref,) = take(1)
-        make_plans(me_ref[0], nqb, nbound, lists, counts, plan, plan_qb, plan_n)
+        make_plans(me_ref[0], nqb, nbound, lists, counts, plan)
         qn_ref[...] = jnp.zeros_like(qn_ref)
         zero = jnp.zeros((64, BLOCK), jnp.bfloat16)
 
@@ -129,22 +124,21 @@
         acc[...] = jnp.zeros_like(acc)
         l_ref[...] = jnp.zeros_like(l_ref)
         qn = jnp.max(qn_ref[...])
-        qn_out[0] = qn
     else:
         acc[...] = acc_in[...]
         l_ref[...] = l_in[...]
         m_ref[...] = m_in[...]
-        qn = qn_in[0]
-
-    for s, tok in enumerate(toks):
-        project(tok, wk, wvt, k_ref, vt_ref, norm_ref, s * (tok.shape[0] // BLOCK))
-    small = qn * jnp.max(norm_ref[...]) <= 3600.0
-    fast = small if kind == FIRST else jnp.logical_and(small, fast_in[0] == 1)
+        qn = jnp.max(m_in[nqb * pairs])
+
+    base = 0
+    for tok in toks:
+        project(tok, wk, wvt, k_ref, vt_ref, norm_ref, base)
+        base += tok.shape[0] // BLOCK
+    fast = jnp.logical_and(qn < 1e20, qn * jnp.max(norm_ref[...]) <= 3600.0)
     if kind == FIRST:
         m_ref[...] = jnp.full_like(m_ref, jnp.where(fast, 0.0, LOW))
-    if kind != LAST:
-        fast_out[0] = fast.astype(jnp.int32)
-    count = plan_n[kind]
+    m_ref[nqb * pairs] = jnp.full_like(m_ref[nqb * pairs], jnp.where(fast, qn, -LOW))
+    count = plan[7, kind]
 
     def blocks(item):
         return jnp.maximum(plan[kind, 2 * item], 0), jnp.maximum(plan[kind, 2 * item + 1], 0)
@@ -153,7 +147,7 @@
         b0, b1 = blocks(item)
         bias0 = jnp.where(plan[kind, 2 * item] < 0, LOW, 0.0).astype(jnp.float32)
         bias1 = jnp.where(plan[kind, 2 * item + 1] < 0, LOW, 0.0).astype(jnp.float32)
-        qb = plan_qb[kind, item]
+        qb = plan[4 + kind, item]
         made = []
         for hp in range(pairs):
             cut = slice(hp * BLOCK, (hp + 1) * BLOCK)
@@ -176,7 +170,7 @@
                     p_ref[slot, hp, i * BLOCK:(i + 1) * BLOCK, :] = jnp.exp(s).astype(jnp.bfloat16)
 
         def gather(item, slot):
-            qb = plan_qb[kind, item]
+            qb = plan[4 + kind, item]
             pvs = [
                 jnp.dot(values(item, hp), p_ref[slot, hp], preferred_element_type=jnp.float32)
                 for hp in range(pairs)
@@ -202,7 +196,7 @@
     @pl.when(jnp.logical_not(fast))
     def _():
         def one(item, carry):
-            qb = plan_qb[kind, item]
+            qb = plan[4 + kind, item]
             for hp, halves in enumerate(scores(item)):
                 row = qb * pairs + hp
                 s = jnp.concatenate(halves, axis=0)
@@ -244,12 +238,12 @@
         nqb = toks[0].shape[0] // BLOCK
     else:
         args += list(state)
-        specs += [smem] * 5 + [vmem] * 4
-        nqb = state[5].shape[0]
+        specs += [smem] + [vmem] * 4
+        nqb = state[1].shape[0]
     if kind == LAST:
         args.append(wo)
         specs.append(vmem)
-    sums = [(nqb * pairs, BLOCK, BLOCK), (nqb * pairs, 1, 2 * BLOCK), (nqb * pairs, 1, 2 * BLOCK)]
+    sums = [(nqb * pairs, BLOCK, BLOCK), (nqb * pairs + 1, 1, 2 * BLOCK), (nqb * pairs, 1, 2 * BLOCK)]
     outs, out_specs, scratch = [], [], []
     if kind == LAST:
         outs.append(jax.ShapeDtypeStruct((nqb * BLOCK, width), jnp.bfloat16))
@@ -257,17 +251,11 @@
         scratch += [pltpu.VMEM(s, jnp.float32) for s in sums]
     else:
         if kind == FIRST:
-            room = nqb * NB + 16
             outs += [
-                jax.ShapeDtypeStruct((4, room), jnp.int32),
-                jax.ShapeDtypeStruct((4, room), jnp.int32),
-                jax.ShapeDtypeStruct((4,), jnp.int32),
-                jax.ShapeDtypeStruct((1,), jnp.float32),
+                jax.ShapeDtypeStruct((8, PLAN_LEN), jnp.int32),
                 jax.ShapeDtypeStruct((nqb, pairs, BLOCK, 2 * BLOCK), jnp.bfloat16),
             ]
-            out_specs += [smem] * 4 + [vmem]
-        outs.append(jax.ShapeDtypeStruct((1,), jnp.int32))
-        out_specs.append(smem)
+            out_specs += [smem, vmem]
         outs += [jax.ShapeDtypeStruct(s, jnp.float32) for s in sums]
         out_specs += [vmem] * 3
     scratch += [
@@ -278,7 +266,7 @@
     ]
     if kind == FIRST:
         scratch.append(pltpu.VMEM((1, ROWS), jnp.float32))
-    units = {FIRST: 18, BOUND: 32, MIDDLE: 34, LAST: 11}[kind]
+    units = {FIRST: 18, MIDDLE: 34, LAST: 43}[kind]
     cost = pl.CostEstimate(
         flops=units * 8 * 2 * BLOCK ** 3 * 8 + nkb * BLOCK * width * width * 4,
         bytes_accessed=8 << 20,
@@ -292,7 +280,7 @@
         scratch_shapes=scratch,
         compiler_params=pltpu.CompilerParams(vmem_limit_bytes=40 << 20),
         cost_estimate=cost,
-        name=("attend_own", "attend_bound", "attend_middle", "attend_last")[kind],
+        name=("attend_own", "attend_middle", "attend_last")[kind],
     )(*args)
 
 
@@ -323,20 +311,9 @@
     wk = w_keyval[:, :width]
     wvt = w_keyval[:, width:].T
     lists = (member.reshape(1).astype(jnp.int32), block_list, block_count)
-    *plan, qn, qbd, fast, acc, top, total = run_phase(
-        FIRST, [tokens], wk, wvt, nbound, lists=lists, wqt=w_query.T
-    )
-
-    slot_range = jnp.arange(nbound, dtype=jnp.int32)
-    owner_start = jnp.sum((owner[None, :] < owner[:, None]).astype(jnp.int32), axis=1)
-    source = owner * BCAP + slot_range - owner_start
-    choose = (source[:, None] == jnp.arange(size * BCAP, dtype=jnp.int32)[None, :]).astype(jnp.bfloat16)
-    bound = jnp.dot(choose, gathered, preferred_element_type=jnp.float32).astype(jnp.bfloat16)
-    fast, acc, top, total = run_phase(
-        BOUND, [bound], wk, wvt, nbound, state=[*plan, fast, qn, qbd, acc, top, total]
-    )
-
-    after = jnp.minimum(fast[0], 0)
+    plan, qbd, *sums = run_phase(FIRST, [tokens], wk, wvt, nbound, lists=lists, wqt=w_query.T)
+
+    after = jnp.minimum(plan[7, 0], 0)
     half = tok_dev // 2
     relay = jnp.where(member % 2 == after, from_two_ahead[:half], from_two_behind[:half])
     low = send(relay, [(i, i ^ 1) for i in everyone])
@@ -344,18 +321,18 @@
     upper = lax.dynamic_slice_in_dim(mate, half + after, half)
     high = send(upper, [(a, b) for a, b in hops if 0 <= b < size])
 
-    fast, acc, top, total = run_phase(
-        MIDDLE,
-        [from_two_behind, from_two_ahead, mate],
-        wk,
-        wvt,
-        nbound,
-        state=[*plan, fast, qn, qbd, acc, top, total],
+    sums = run_phase(
+        MIDDLE, [from_two_behind, from_two_ahead, mate], wk, wvt, nbound, state=[plan, qbd, *sums]
     )
+
+    slot_range = jnp.arange(nbound, dtype=jnp.int32)
+    owner_start = jnp.sum((owner[None, :] < owner[:, None]).astype(jnp.int32), axis=1)
+    done = (sums[1][-1, 0, 0] < LOW).astype(jnp.int32)
+    source = owner * BCAP + slot_range - owner_start + done
+    choose = (source[:, None] == jnp.arange(size * BCAP, dtype=jnp.int32)[None, :]).astype(jnp.bfloat16)
+    bound = jnp.dot(choose, gathered, preferred_element_type=jnp.float32).astype(jnp.bfloat16)
     far = jnp.concatenate([low, high], axis=0)
-    (mixed,) = run_phase(
-        LAST, [far], wk, wvt, nbound, state=[*plan, fast, qn, qbd, acc, top, total], wo=w_out
-    )
+    (mixed,) = run_phase(LAST, [far, bound], wk, wvt, nbound, state=[plan, qbd, *sums], wo=w_out)
     return mixed
 
 

time: 132 us -> 115 us (0.87)
  the two profiles are of different devices: /device:TPU:15 before, /device:TPU:8 now
where the time goes in v1:
time: 115 us; the launch traced here: 114 us
  Pallas kernels  64.3 us (56%)
  between operations  16.8 us (15%)
  starting transfers between devices  13.7 us (12%)
  local copies, waits for them, and re-layouts  11.2 us (10%)
  matrix products  4.42 us (4%)
  other arithmetic  3.81 us (3%)
    pallas_call x3, Pallas kernels, run_phase(): pl.pallas_call(functools.partial(phase, kind, len(toks), nbound), out_sha...  64.3 us
    ppermute x5, starting transfers between devices, send(): return lax.ppermute(value, 'curve', pairs)  13.7 us
    unnamed x26, local copies, waits for them, and re-layouts  7.61 us
  transfers between devices with their start and end apart: 6, of which 0 were waited for; matrix products, arithmetic and copies ran while one was open for 9% of the time, Pallas kernels for 37%

profile of v1, /device:TPU:8, one launch (start us, length us, event | category | flops | bytes accessed | tf_op | source)
XLA Modules:
  0.0 114.3 jit_solution(6315856326855936368)
XLA Ops:
  6.5 0.0 all-gather.2.cloned.1.call-start
  6.5 1.9 %collective-permute-start = (bf16[1024,512]{1,0:T(8,128)(2,1)}, bf16[1024,512]{1,0:T(8,128)(2,1)}, u32[]{:S(2)}, u32[]{:S(2)}) collective-permute-start(bf16[1024,512]{1,0:T(8,128)(2,1)} %refs_0_.1), channel_id=1, source_target_pairs={{2,0},{3,1},{4,2},{5,3},{6,4},{7,5},{10,8},{11,9},{12,10},{13,11},... | collective-permute-start | bytes 3145736 | tf_op jit(solution)/shard_map/ppermute | solution.py:288
  8.5 3.9 %collective-permute-start.1 = (bf16[1024,512]{1,0:T(8,128)(2,1)}, bf16[1024,512]{1,0:T(8,128)(2,1)}, u32[]{:S(2)}, u32[]{:S(2)}) collective-permute-start(bf16[1024,512]{1,0:T(8,128)(2,1)} %refs_0_.1), channel_id=1, source_target_pairs={{0,2},{1,3},{2,4},{3,5},{4,6},{5,7},{8,10},{9,11},{10,12},{11,13},... | collective-permute-start | bytes 3145736 | tf_op jit(solution)/shard_map/ppermute | solution.py:288
  12.4 1.6 %collective-permute-start.3 = (bf16[1024,512]{1,0:T(8,128)(2,1)}, bf16[1024,512]{1,0:T(8,128)(2,1)}, u32[]{:S(2)}, u32[]{:S(2)}) collective-permute-start(bf16[1024,512]{1,0:T(8,128)(2,1)} %refs_0_.1), channel_id=1, source_target_pairs={{0,1},{1,0},{2,3},{3,2},{4,5},{5,4},{6,7},{7,6},{8,9},{9,8},{10,11... | collective-permute-start | bytes 3145736 | tf_op jit(solution)/shard_map/ppermute | solution.py:288
  14.0 1.3 %convert_reduce_fusion.1 = (s32[]{:T(128)}, s32[512]{0:T(512)S(1)}) fusion(s32[]{:T(128)} %axis_index.12, s32[512]{0:T(512)} %param.13), kind=kLoop, calls=%fused_computation.16 | loop fusion | flops 9215 | bytes 4104 | tf_op jit(solution)/shard_map/reduce_sum | solution.py:300
  17.2 0.8 fusion.6
  18.0 0.0 copy-start.11
  18.0 2.3 %convolution_convert_fusion = bf16[128,512]{1,0:T(8,128)(2,1)} fusion(bf16[1024,512]{1,0:T(8,128)(2,1)} %refs_0_.1, s32[128]{0:T(128)S(1)} %fusion.6), kind=kOutput, calls=%fused_computation.3 | convolution fusion | flops 134414336 | bytes 1180160 | tf_op jit(solution)/shard_map/dot_general | solution.py:304
  20.3 0.0 all-gather.2.cloned.1.call-update
  20.3 0.0 copy-start
  20.3 0.0 copy-start.2
  20.4 0.0 copy-start.3
  20.4 1.4 %fusion.7 = (bf16[512,512]{1,0:T(8,128)(2,1)S(1)}, bf16[512,512]{1,0:T(8,128)(2,1)S(1)}) fusion(bf16[512,1024]{1,0:T(8,128)(2,1)} %param.9), kind=kLoop, calls=%fused_computation.22 | loop fusion | bytes 2097152 | tf_op jit(solution)/shard_map/slice | solution.py:312
  21.7 0.2 copy.12
  21.9 0.0 copy-done.11
  22.0 0.2 copy.11
  22.2 0.0 copy-done
  22.2 0.0 copy-done.2
  22.2 0.0 copy-done.3
  22.2 16.9 %attend_own.1 = (s32[8,128]{1,0:T(8,128)S(1)}, bf16[8,4,128,256]{3,2,1,0:T(8,128)(2,1)S(1)}, f32[32,128,128]{2,1,0:T(8,128)S(1)}, f32[33,1,256]{2,1,0:T(1,128)S(1)}, f32[32,1,256]{2,1,0:T(1,128)S(1)}) custom-call(bf16[1024,512]{1,0:T(8,128)(2,1)S(1)} %copy-done, bf16[512,512]{1,0:T(8,128)(2,1)S(1)} %get-tuple-element.24.refs_1_.refs_3_.refs_2_, ...), custom_call_target="tpu_custom_call" | custom-call | flops 5905580032 | bytes 8388608 | tf_op jit(solution)/shard_map/attend_own/pallas_call | solution.py:275
  39.1 0.0 copy-start.4
  39.1 1.3 %copy-done.4 = bf16[8,4,128,256]{3,2,1,0:T(8,128)(2,1)} copy-done((bf16[8,4,128,256]{3,2,1,0:T(8,128)(2,1)}, bf16[8,4,128,256]{3,2,1,0:T(8,128)(2,1)S(1)}, u32[]{:S(2)}) %copy-start.4) | copy-done | bytes 2097176
  40.5 0.0 copy-start.7
  40.5 1.3 %copy-done.7 = f32[32,128,128]{2,1,0:T(8,128)} copy-done((f32[32,128,128]{2,1,0:T(8,128)}, f32[32,128,128]{2,1,0:T(8,128)S(1)}, u32[]{:S(2)}) %copy-start.7) | copy-done | bytes 2097176
  41.8 0.5 slice.20
  42.8 0.0 copy-start.5
  42.9 0.2 convert_reduce_fusion
  43.1 0.0 collective-permute-done.refs_1_
  43.1 0.0 collective-permute-done.1.refs_0_
  43.1 1.4 %slice_select_fusion = bf16[512,512]{1,0:T(8,128)(2,1)S(1)} fusion(bf16[1024,512]{1,0:T(8,128)(2,1)} %collective-permute-done.1.refs_0_, bf16[1024,512]{1,0:T(8,128)(2,1)} %collective-permute-done.refs_1_, pred[]{:T(512)S(6)} %eq.16), kind=kLoop, calls=%fused_computation.7 | loop fusion | flops 262144 | bytes 1572865 | tf_op jit(solution)/shard_map/jit(_where)/select_n | solution.py:318
  44.5 3.1 %collective-permute-start.2 = (bf16[512,512]{1,0:T(8,128)(2,1)S(1)}, bf16[512,512]{1,0:T(8,128)(2,1)S(1)}, u32[]{:S(2)}, u32[]{:S(2)}) collective-permute-start(bf16[512,512]{1,0:T(8,128)(2,1)S(1)} %slice_select_fusion), channel_id=1, source_target_pairs={{0,1},{1,0},{2,3},{3,2},{4,5},{5,4},{6,7},{7,6},{8,9},{9,8},{10,11... | collective-permute-start | bytes 1572872 | tf_op jit(solution)/shard_map/ppermute | solution.py:288
  47.6 0.0 collective-permute-done.3.refs_2_
  47.6 1.2 %constant_dynamic-slice_fusion = bf16[512,512]{1,0:T(8,128)(2,1)S(1)} fusion(bf16[1024,512]{1,0:T(8,128)(2,1)} %collective-permute-done.3.refs_2_, s32[]{:T(128)S(6)} %select_n.29), kind=kLoop, calls=%fused_computation.21 | loop fusion | bytes 1048580 | tf_op jit(solution)/shard_map/dynamic_slice | solution.py:321
  48.8 3.2 %collective-permute-start.4 = (bf16[512,512]{1,0:T(8,128)(2,1)S(1)}, bf16[512,512]{1,0:T(8,128)(2,1)S(1)}, u32[]{:S(2)}, u32[]{:S(2)}) collective-permute-start(bf16[512,512]{1,0:T(8,128)(2,1)S(1)} %constant_dynamic-slice_fusion), channel_id=1, source_target_pairs={{0,2},{2,4},{3,1},{4,6},{5,3},{7,5},{8,10},{10,12},{11,9},{12,14},... | collective-permute-start | bytes 1572872 | tf_op jit(solution)/shard_map/ppermute | solution.py:288
  52.0 0.0 copy-done.5
  52.0 0.0 copy-start.8
  52.0 1.6 %copy-done.8 = f32[32,128,128]{2,1,0:T(8,128)S(1)} copy-done((f32[32,128,128]{2,1,0:T(8,128)S(1)}, f32[32,128,128]{2,1,0:T(8,128)}, u32[]{:S(2)}) %copy-start.8) | copy-done | bytes 2097176
  53.6 24.8 %attend_middle.1 = (f32[32,128,128]{2,1,0:T(8,128)S(1)}, f32[33,1,256]{2,1,0:T(1,128)S(1)}, f32[32,1,256]{2,1,0:T(1,128)S(1)}) custom-call(bf16[1024,512]{1,0:T(8,128)(2,1)} %collective-permute-done.1.refs_0_, bf16[1024,512]{1,0:T(8,128)(2,1)} %collective-permute-done.refs_1_, bf16[1024,512]{1,0:T(8,128)(2,1)} %collective-permute-done.3.refs_2_, ...), custom_call_target="tpu_custom_call" | custom-call | flops 12348030976 | bytes 8388608 | tf_op jit(solution)/shard_map/attend_middle/pallas_call | solution.py:275
  78.5 0.0 copy-start.9
  78.5 1.3 %copy-done.9 = f32[32,128,128]{2,1,0:T(8,128)} copy-done((f32[32,128,128]{2,1,0:T(8,128)}, f32[32,128,128]{2,1,0:T(8,128)S(1)}, u32[]{:S(2)}) %copy-start.9) | copy-done | bytes 2097176
  79.8 0.6 slice.23
  81.0 0.0 collective-permute-done.2
  81.0 0.0 collective-permute-done.4
  81.0 0.1 pad_maximum_fusion.refs_0_
  81.1 0.0 copy-start.1
  81.1 0.0 all-gather.2.cloned.1.call-done
  81.1 0.0 copy-start.6
  81.2 2.1 %fusion.1.refs_1_ = bf16[512,512]{1,0:T(8,128)(2,1)S(1)} fusion(bf16[1024,512]{1,0:T(8,128)(2,1)} %all-gather.2.cloned.1.call-done, s32[512]{0:T(512)S(1)} %subtract_add_fusion), kind=kOutput, calls=%fused_computation.2 | convolution fusion | flops 537657344 | bytes 1574912 | tf_op jit(solution)/shard_map/dot_general | solution.py:333
  83.3 0.0 copy-done.1
  83.3 0.0 copy-done.6
  83.3 0.0 copy-start.10
  83.3 1.6 %copy-done.10 = f32[32,128,128]{2,1,0:T(8,128)S(1)} copy-done((f32[32,128,128]{2,1,0:T(8,128)S(1)}, f32[32,128,128]{2,1,0:T(8,128)}, u32[]{:S(2)}) %copy-start.10) | copy-done | bytes 2097176
  84.9 22.6 %attend_last.1 = bf16[1024,512]{1,0:T(8,128)(2,1)} custom-call(bf16[1024,512]{1,0:T(8,128)(2,1)S(1)} %pad_maximum_fusion.refs_0_, bf16[512,512]{1,0:T(8,128)(2,1)S(1)} %fusion.1.refs_1_, bf16[512,512]{1,0:T(8,128)(2,1)S(1)} %get-tuple-element.24.refs_1_.refs_3_.refs_2_, bf16[512,512]{1,0:T(8,128)(2,1)S(1)} %bitcast.9, ...), custom_call_target="tpu_custom_call" | custom-call | flops 13153337344 | bytes 8388608 | tf_op jit(solution)/shard_map/attend_last/pallas_call | solution.py:275
  (1 shorter events, 0.0 us)
Async XLA Ops:
  6.5 74.6 %all-gather.2.cloned.1.call-start = ((), (), s32[]{:S(2)}) async-start(), calls=%async_computation | async-start | bytes 1179648 | tf_op jit(solution)/shard_map/all_gather | solution.py:305
  6.5 36.6 %collective-permute-start = (bf16[1024,512]{1,0:T(8,128)(2,1)}, bf16[1024,512]{1,0:T(8,128)(2,1)}, u32[]{:S(2)}, u32[]{:S(2)}) collective-permute-start(bf16[1024,512]{1,0:T(8,128)(2,1)} %refs_0_.1), channel_id=1, source_target_pairs={{2,0},{3,1},{4,2},{5,3},{6,4},{7,5},{10,8},{11,9},{12,10},{13,11},... | collective-permute-start | bytes 3145736 | tf_op jit(solution)/shard_map/ppermute | solution.py:288
  8.5 34.7 %collective-permute-start.1 = (bf16[1024,512]{1,0:T(8,128)(2,1)}, bf16[1024,512]{1,0:T(8,128)(2,1)}, u32[]{:S(2)}, u32[]{:S(2)}) collective-permute-start(bf16[1024,512]{1,0:T(8,128)(2,1)} %refs_0_.1), channel_id=1, source_target_pairs={{0,2},{1,3},{2,4},{3,5},{4,6},{5,7},{8,10},{9,11},{10,12},{11,13},... | collective-permute-start | bytes 3145736 | tf_op jit(solution)/shard_map/ppermute | solution.py:288
  12.4 35.2 %collective-permute-start.3 = (bf16[1024,512]{1,0:T(8,128)(2,1)}, bf16[1024,512]{1,0:T(8,128)(2,1)}, u32[]{:S(2)}, u32[]{:S(2)}) collective-permute-start(bf16[1024,512]{1,0:T(8,128)(2,1)} %refs_0_.1), channel_id=1, source_target_pairs={{0,1},{1,0},{2,3},{3,2},{4,5},{5,4},{6,7},{7,6},{8,9},{9,8},{10,11... | collective-permute-start | bytes 3145736 | tf_op jit(solution)/shard_map/ppermute | solution.py:288
  18.0 3.9 %copy-start.11 = (bf16[512,512]{1,0:T(8,128)(2,1)S(1)}, bf16[512,512]{1,0:T(8,128)(2,1)}, u32[]{:S(2)}) copy-start(bf16[512,512]{1,0:T(8,128)(2,1)} %param.8) | copy-start | bytes 1572868
  20.3 1.8 %copy-start = (bf16[1024,512]{1,0:T(8,128)(2,1)S(1)}, bf16[1024,512]{1,0:T(8,128)(2,1)}, u32[]{:S(2)}) copy-start(bf16[1024,512]{1,0:T(8,128)(2,1)} %refs_0_.1) | copy-start | bytes 3145732
  20.3 1.8 %copy-start.2 = (s32[8,12]{1,0:T(8,128)S(1)}, s32[8,12]{1,0:T(8,128)}, u32[]{:S(2)}) copy-start(s32[8,12]{1,0:T(8,128)} %refs_4_.1) | copy-start | bytes 1156
  20.4 1.8 %copy-start.3 = (s32[8]{0:T(128)S(1)}, s32[8]{0:T(128)}, u32[]{:S(2)}) copy-start(s32[8]{0:T(128)} %refs_5_.1) | copy-start | bytes 100
  39.1 1.3 %copy-start.4 = (bf16[8,4,128,256]{3,2,1,0:T(8,128)(2,1)}, bf16[8,4,128,256]{3,2,1,0:T(8,128)(2,1)S(1)}, u32[]{:S(2)}) copy-start(bf16[8,4,128,256]{3,2,1,0:T(8,128)(2,1)S(1)} %get-tuple-element.14.refs_6_.refs_5_) | copy-start | bytes 6291460
  40.5 1.3 %copy-start.7 = (f32[32,128,128]{2,1,0:T(8,128)}, f32[32,128,128]{2,1,0:T(8,128)S(1)}, u32[]{:S(2)}) copy-start(f32[32,128,128]{2,1,0:T(8,128)S(1)} %get-tuple-element.15.refs_7_) | copy-start | bytes 6291460
  42.8 9.2 %copy-start.5 = (bf16[8,4,128,256]{3,2,1,0:T(8,128)(2,1)S(1)}, bf16[8,4,128,256]{3,2,1,0:T(8,128)(2,1)}, u32[]{:S(2)}) copy-start(bf16[8,4,128,256]{3,2,1,0:T(8,128)(2,1)} %copy-done.4) | copy-start | bytes 6291460
  44.5 36.5 %collective-permute-start.2 = (bf16[512,512]{1,0:T(8,128)(2,1)S(1)}, bf16[512,512]{1,0:T(8,128)(2,1)S(1)}, u32[]{:S(2)}, u32[]{:S(2)}) collective-permute-start(bf16[512,512]{1,0:T(8,128)(2,1)S(1)} %slice_select_fusion), channel_id=1, source_target_pairs={{0,1},{1,0},{2,3},{3,2},{4,5},{5,4},{6,7},{7,6},{8,9},{9,8},{10,11... | collective-permute-start | bytes 1572872 | tf_op jit(solution)/shard_map/ppermute | solution.py:288
  48.8 32.3 %collective-permute-start.4 = (bf16[512,512]{1,0:T(8,128)(2,1)S(1)}, bf16[512,512]{1,0:T(8,128)(2,1)S(1)}, u32[]{:S(2)}, u32[]{:S(2)}) collective-permute-start(bf16[512,512]{1,0:T(8,128)(2,1)S(1)} %constant_dynamic-slice_fusion), channel_id=1, source_target_pairs={{0,2},{2,4},{3,1},{4,6},{5,3},{7,5},{8,10},{10,12},{11,9},{12,14},... | collective-permute-start | bytes 1572872 | tf_op jit(solution)/shard_map/ppermute | solution.py:288
  52.0 1.6 %copy-start.8 = (f32[32,128,128]{2,1,0:T(8,128)S(1)}, f32[32,128,128]{2,1,0:T(8,128)}, u32[]{:S(2)}) copy-start(f32[32,128,128]{2,1,0:T(8,128)} %copy-done.7) | copy-start | bytes 6291460
  78.5 1.3 %copy-start.9 = (f32[32,128,128]{2,1,0:T(8,128)}, f32[32,128,128]{2,1,0:T(8,128)S(1)}, u32[]{:S(2)}) copy-start(f32[32,128,128]{2,1,0:T(8,128)S(1)} %get-tuple-element.19.refs_6_) | copy-start | bytes 6291460
  81.1 2.2 %copy-start.1 = (bf16[512,512]{1,0:T(8,128)(2,1)S(1)}, bf16[512,512]{1,0:T(8,128)(2,1)}, u32[]{:S(2)}) copy-start(bf16[512,512]{1,0:T(8,128)(2,1)} %refs_9_.1) | copy-start | bytes 1572868
  81.1 2.2 %copy-start.6 = (bf16[8,4,128,256]{3,2,1,0:T(8,128)(2,1)S(1)}, bf16[8,4,128,256]{3,2,1,0:T(8,128)(2,1)}, u32[]{:S(2)}) copy-start(bf16[8,4,128,256]{3,2,1,0:T(8,128)(2,1)} %copy-done.4) | copy-start | bytes 6291460
  83.3 1.6 %copy-start.10 = (f32[32,128,128]{2,1,0:T(8,128)S(1)}, f32[32,128,128]{2,1,0:T(8,128)}, u32[]{:S(2)}) copy-start(f32[32,128,128]{2,1,0:T(8,128)} %copy-done.9) | copy-start | bytes 6291460
Sparse Core Ops, SparseCore 0:
  20.5 46.4 all-gather.1

commit v2 on v1

v2 whole, which is shorter than its diff:
```python
import functools

import jax
import jax.numpy as jnp
from jax import lax
from jax.experimental import pallas as pl
from jax.experimental.pallas import tpu as pltpu
from jax.sharding import PartitionSpec as P

HEADS = 8
BLOCK = 128
NB = 12
BCAP = 128
LOW = -1e30
ROWS = 256

FIRST, MIDDLE, LAST = range(3)
PLAN_LEN = 128


def cast_dot(a, b, dims):
    out = lax.dot_general(a, b, (dims, ((), ())), preferred_element_type=jnp.float32)
    return out.astype(jnp.bfloat16)


def project(tok, wk, wvt, k_ref, vt_ref, norm_ref, base):
    width = wvt.shape[0]
    feature = lax.broadcasted_iota(jnp.int32, (width, BLOCK), 0)
    head = lax.broadcasted_iota(jnp.int32, (width, BLOCK), 1)
    ind = jnp.where(feature >> 6 == head, 1.0, 0.0).astype(jnp.bfloat16)

    @pl.loop(0, tok.shape[0] // ROWS)
    def _(t):
        rows = tok[pl.ds(pl.multiple_of(t * ROWS, ROWS), ROWS), :]
        k = cast_dot(rows, wk[:, :width], ((1,), (0,)))
        vt = cast_dot(wvt[...], rows, ((1,), (1,)))
        for i in range(ROWS // BLOCK):
            at = base + t * (ROWS // BLOCK) + i
            k_ref[at] = k[i * BLOCK:(i + 1) * BLOCK, :]
            vt_ref[at] = vt[:, i * BLOCK:(i + 1) * BLOCK]
        norm = jnp.dot(k * k, ind, preferred_element_type=jnp.float32)
        norm_ref[...] = jnp.maximum(norm_ref[...], jnp.max(norm, axis=0, keepdims=True))


def plan_row(me, nqb, nbound, lists, counts, plan, qb, tops):
    used = counts[qb]
    near = 3 - 2 * lax.rem(me, 2)
    ns = list(tops)
    for i in range(NB):
        rel = jnp.clip(lists[qb, i] - (me - 2) * nqb, 0, 5 * nqb - 1)
        slot = lax.div(rel, nqb)
        src = jnp.where(slot == 4, 1, jnp.where(slot == near, 2, 0))
        block = src * nqb + rel - slot * nqb
        last = slot == 4 - near
        own = slot == 2
        live = (i < used).astype(jnp.int32)
        kind = jnp.where(own, FIRST, jnp.where(last, LAST, MIDDLE))
        for k in (FIRST, MIDDLE, LAST):
            plan[k, ns[k]] = block
            ns[k] = ns[k] + jnp.where(kind == k, live, 0)
    for k in (FIRST, MIDDLE, LAST):
        plan[k, ns[k]] = -1
        top = tops[k] + 2 * lax.div(ns[k] - tops[k] + 1, 2)
        if k == LAST:
            for j in range(nbound // BLOCK):
                plan[k, top + j] = nqb + j
            top = top + nbound // BLOCK
        first = lax.div(tops[k], 2)
        for j in range((NB + nbound // BLOCK) // 2 if k == LAST else NB // 2):
            plan[4 + k, first + j] = qb
        ns[k] = top
    return tuple(ns)


def plan_end(plan, tops):
    for k in (FIRST, MIDDLE, LAST):
        plan[k, tops[k]] = -1
        plan[k, tops[k] + 1] = -1
        plan[4 + k, lax.div(tops[k], 2)] = 0
        plan[7, k] = lax.div(tops[k] + 2, 4)


def pick_rows(me_ref, ids, tokens, out):
    me, tok_dev = me_ref[0], tokens.shape[0]
    n = ids.shape[1]
    mine = ids[...]
    start = jnp.sum(jnp.where(mine < me * tok_dev, 1.0, 0.0), axis=1, keepdims=True).astype(jnp.int32)
    r = lax.broadcasted_iota(jnp.int32, (BCAP, n), 0)
    j = lax.broadcasted_iota(jnp.int32, (BCAP, n), 1)
    local = (mine - me * tok_dev).astype(jnp.float32)
    spot = jnp.sum(jnp.where(j - r == start, local, 0.0), axis=1, keepdims=True).astype(jnp.int32)
    t = lax.broadcasted_iota(jnp.int32, (BCAP, tok_dev), 1)
    chosen = jnp.where(t == spot, 1.0, 0.0).astype(jnp.bfloat16)
    out[...] = cast_dot(chosen, tokens[...], ((1,), (0,)))


def join_rows(ids, gathered, out, tok_dev):
    n = ids.shape[1]
    size = gathered.shape[0] // BCAP
    mine = ids[...]
    j = lax.broadcasted_iota(jnp.int32, (n, BCAP), 0)
    r = lax.broadcasted_iota(jnp.int32, (n, BCAP), 1)
    starts = [
        jnp.sum(jnp.where(mine < o * tok_dev, 1.0, 0.0), axis=1, keepdims=True).astype(jnp.int32)
        for o in range(size + 1)
    ]
    parts = []
    for o in range(size):
        hit = jnp.logical_and(j - r == starts[o], r < starts[o + 1] - starts[o])
        parts.append(jnp.where(hit, 1.0, 0.0).astype(jnp.bfloat16))
    out[...] = cast_dot(jnp.concatenate(parts, axis=1), gathered[...], ((1,), (0,)))


def phase(kind, nsrc, nbound, *refs):
    refs = list(refs)
    take = lambda n: [refs.pop(0) for _ in range(n)]
    toks = take(nsrc)
    (wk,) = take(1)
    if kind == FIRST:
        me_ref, lists, counts, wq = take(4)
    else:
        wvt, plan, qbd, acc_in, m_in, l_in = take(6)
    if kind == LAST:
        ids, gathered, wo, out = take(4)
    elif kind == FIRST:
        wvt, plan, qbd = take(3)
    acc, m_ref, l_ref, k_ref, vt_ref, p_ref, norm_ref = take(7)
    nqb, pairs = qbd.shape[0], qbd.shape[1]

    norm_ref[...] = jnp.zeros_like(norm_ref)
    if kind == FIRST:
        qn_ref, wqt = take(2)
        wqt[...] = wq[...].T
        wvt[...] = wk[:, wvt.shape[0]:].T
        qn_ref[...] = jnp.zeros_like(qn_ref)
        zero = jnp.zeros((64, BLOCK), jnp.bfloat16)

        def query(t, tops):
            rows = toks[0][pl.ds(pl.multiple_of(t * ROWS, ROWS), ROWS), :]
            q = lax.dot_general(wqt[...], rows, (((1,), (1,)), ((), ())), preferred_element_type=jnp.float32)
            q = q.astype(jnp.bfloat16) * jnp.bfloat16(0.125)
            for i in range(ROWS // BLOCK):
                for hp in range(pairs):
                    cut = q[hp * BLOCK:(hp + 1) * BLOCK, i * BLOCK:(i + 1) * BLOCK]
                    at = t * (ROWS // BLOCK) + i
                    qbd[at, hp, :64, :] = jnp.concatenate([cut[:64], zero], axis=1)
                    qbd[at, hp, 64:, :] = jnp.concatenate([zero, cut[64:]], axis=1)
            q = q.astype(jnp.float32)
            for h in range(2 * pairs):
                part = q[h * 64:(h + 1) * 64, :]
                qn_ref[...] = jnp.maximum(qn_ref[...], jnp.sum(part * part, axis=0, keepdims=True))
            for i in range(ROWS // BLOCK):
                qb = t * (ROWS // BLOCK) + i
                tops = plan_row(me_ref[0], nqb, nbound, lists, counts, plan, qb, tops)
            return tops

        tops = lax.fori_loop(0, toks[0].shape[0] // ROWS, query, (jnp.int32(0),) * 3)
        plan_end(plan, tops)
        acc[...] = jnp.zeros_like(acc)
        l_ref[...] = jnp.zeros_like(l_ref)
        qn = jnp.max(qn_ref[...])
    else:
        acc[...] = acc_in[...]
        l_ref[...] = l_in[...]
        m_ref[...] = m_in[...]
        qn = jnp.max(m_in[nqb * pairs])

    base = 0
    if kind == LAST:
        (bound,) = take(1)
        join_rows(ids, gathered, bound, toks[0].shape[0])
        toks = toks + [bound]
    for tok in toks:
        project(tok, wk, wvt, k_ref, vt_ref, norm_ref, base)
        base += tok.shape[0] // BLOCK
    fast = jnp.logical_and(qn < 1e20, qn * jnp.max(norm_ref[...]) <= 3600.0)
    if kind == FIRST:
        m_ref[...] = jnp.full_like(m_ref, jnp.where(fast, 0.0, LOW))
    m_ref[nqb * pairs] = jnp.full_like(m_ref[nqb * pairs], jnp.where(fast, qn, -LOW))
    count = plan[7, kind]

    def blocks(item):
        return jnp.maximum(plan[kind, 2 * item], 0), jnp.maximum(plan[kind, 2 * item + 1], 0)

    def scores(item):
        b0, b1 = blocks(item)
        qb = plan[4 + kind, item]
        made = []
        for hp in range(pairs):
            cut = slice(hp * BLOCK, (hp + 1) * BLOCK)
            k = jnp.concatenate([k_ref[b0, :, cut], k_ref[b1, :, cut]], axis=0)
            made.append(jnp.dot(k, qbd[qb, hp], preferred_element_type=jnp.float32))
        return made

    def values(item, hp):
        b0, b1 = blocks(item)
        cut = slice(hp * BLOCK, (hp + 1) * BLOCK)
        halves = []
        for b, live in ((b0, plan[kind, 2 * item] >= 0), (b1, plan[kind, 2 * item + 1] >= 0)):
            v = jnp.concatenate([vt_ref[b, cut, :], jnp.ones((16, BLOCK), jnp.bfloat16)], axis=0)
            halves.append(v * jnp.where(live, 1.0, 0.0).astype(jnp.bfloat16))
        return jnp.concatenate(halves, axis=1)

    @pl.when(fast)
    def _():
        def weigh(item, slot):
            for hp, s in enumerate(scores(item)):
                p_ref[slot, hp] = jnp.exp(s).astype(jnp.bfloat16)

        def gather(item, slot):
            qb = plan[4 + kind, item]
            pvs = [
                jnp.dot(values(item, hp), p_ref[slot, hp], preferred_element_type=jnp.float32)
                for hp in range(pairs)
            ]
            for hp, pv in enumerate(pvs):
                row = qb * pairs + hp
                acc[row, :64, :] = acc[row, :64, :] + pv[:64, :BLOCK]
                acc[row, 64:, :] = acc[row, 64:, :] + pv[64:BLOCK, BLOCK:]
                l_ref[row] = l_ref[row] + pv[BLOCK:BLOCK + 1, :]

        p_ref[1] = jnp.zeros_like(p_ref[1])

        def two(t, carry):
            gather(jnp.maximum(2 * t - 1, 0), 1)
            weigh(2 * t, 0)
            gather(2 * t, 0)
            weigh(2 * t + 1, 1)
            return carry

        lax.fori_loop(0, count, two, 0)
        gather(jnp.maximum(2 * count - 1, 0), 1)

    @pl.when(jnp.logical_not(fast))
    def _():
        def one(item, carry):
            qb = plan[4 + kind, item]
            bias0 = jnp.where(plan[kind, 2 * item] < 0, LOW, 0.0).astype(jnp.float32)
            bias1 = jnp.where(plan[kind, 2 * item + 1] < 0, LOW, 0.0).astype(jnp.float32)
            for hp, s in enumerate(scores(item)):
                row = qb * pairs + hp
                s = jnp.concatenate([s[:BLOCK] + bias0, s[BLOCK:] + bias1], axis=0)
                m_old = m_ref[row]
                m_new = jnp.maximum(m_old, jnp.max(s, axis=0, keepdims=True))
                p = jnp.exp(s - m_new).astype(jnp.bfloat16)
                alpha = jnp.exp(m_old - m_new)
                pv = jnp.dot(values(item, hp), p, preferred_element_type=jnp.float32)
                acc[row, :64, :] = acc[row, :64, :] * alpha[:, :BLOCK] + pv[:64, :BLOCK]
                acc[row, 64:, :] = acc[row, 64:, :] * alpha[:, BLOCK:] + pv[64:BLOCK, BLOCK:]
                l_ref[row] = l_ref[row] * alpha + pv[BLOCK:BLOCK + 1, :]
                m_ref[row] = m_new
            return carry

        lax.fori_loop(0, 2 * count, one, 0)

    if kind == LAST:
        @pl.loop(0, nqb)
        def _(qb):
            parts = []
            for hp in range(pairs):
                row = qb * pairs + hp
                inv = 1.0 / l_ref[row]
                parts.append(acc[row, :64, :] * inv[:, :BLOCK])
                parts.append(acc[row, 64:, :] * inv[:, BLOCK:])
            ctx = jnp.concatenate(parts, axis=0).T.astype(jnp.bfloat16)
            out[pl.ds(pl.multiple_of(qb * BLOCK, BLOCK), BLOCK), :] = cast_dot(ctx, wo[...], ((1,), (0,)))


def run_phase(kind, toks, wk, nbound, lists=None, wq=None, state=None, ends=None):
    width = wk.shape[0]
    pairs = width // BLOCK
    nkb = sum(t.shape[0] for t in toks) // BLOCK + (nbound // BLOCK if kind == LAST else 0)
    vmem, smem = pl.BlockSpec(memory_space=pltpu.VMEM), pl.BlockSpec(memory_space=pltpu.SMEM)
    args, specs = list(toks) + [wk], [vmem] * (len(toks) + 1)
    if kind == FIRST:
        args += list(lists) + [wq]
        specs += [smem] * 3 + [vmem]
        nqb = toks[0].shape[0] // BLOCK
    else:
        args += list(state)
        specs += [vmem, smem] + [vmem] * 4
        nqb = state[2].shape[0]
    if kind == LAST:
        args += list(ends)
        specs += [vmem] * 3
    sums = [(nqb * pairs, BLOCK, BLOCK), (nqb * pairs + 1, 1, 2 * BLOCK), (nqb * pairs, 1, 2 * BLOCK)]
    outs, out_specs, scratch = [], [], []
    if kind == LAST:
        outs.append(jax.ShapeDtypeStruct((nqb * BLOCK, width), jnp.bfloat16))
        out_specs.append(vmem)
        scratch += [pltpu.VMEM(s, jnp.float32) for s in sums]
    else:
        if kind == FIRST:
            outs += [
                jax.ShapeDtypeStruct((width, width), jnp.bfloat16),
                jax.ShapeDtypeStruct((8, PLAN_LEN), jnp.int32),
                jax.ShapeDtypeStruct((nqb, pairs, BLOCK, 2 * BLOCK), jnp.bfloat16),
            ]
            out_specs += [vmem, smem, vmem]
        outs += [jax.ShapeDtypeStruct(s, jnp.float32) for s in sums]
        out_specs += [vmem] * 3
    scratch += [
        pltpu.VMEM((nkb, BLOCK, width), jnp.bfloat16),
        pltpu.VMEM((nkb, width, BLOCK), jnp.bfloat16),
        pltpu.VMEM((2, pairs, 2 * BLOCK, 2 * BLOCK), jnp.bfloat16),
        pltpu.VMEM((1, BLOCK), jnp.float32),
    ]
    if kind == FIRST:
        scratch += [pltpu.VMEM((1, ROWS), jnp.float32), pltpu.VMEM((width, width), jnp.bfloat16)]
    if kind == LAST:
        scratch.append(pltpu.VMEM((nbound, width), jnp.bfloat16))
    units = {FIRST: 18, MIDDLE: 34, LAST: 43}[kind]
    cost = pl.CostEstimate(
        flops=units * 8 * 2 * BLOCK ** 3 * 8 + nkb * BLOCK * width * width * 4,
        bytes_accessed=8 << 20,
        transcendentals=units * 8 * BLOCK * BLOCK,
    )
    return pl.pallas_call(
        functools.partial(phase, kind, len(toks), nbound),
        out_shape=outs,
        in_specs=specs,
        out_specs=out_specs,
        scratch_shapes=scratch,
        compiler_params=pltpu.CompilerParams(vmem_limit_bytes=24 << 20),
        cost_estimate=cost,
        name=("attend_own", "attend_middle", "attend_last")[kind],
    )(*args)


def send(value, pairs):
    return lax.ppermute(value, "curve", pairs)


def on_device(tokens, w_query, w_keyval, w_out, block_list, block_count, bnd_ids):
    tok_dev, width = tokens.shape
    nbound = bnd_ids.shape[0]
    size = lax.axis_size("curve")
    member = lax.axis_index("curve")
    everyone = range(size)

    vmem, smem = pl.BlockSpec(memory_space=pltpu.VMEM), pl.BlockSpec(memory_space=pltpu.SMEM)
    me = member.reshape(1).astype(jnp.int32)
    ids = bnd_ids.reshape(1, nbound)
    rows = pl.pallas_call(
        pick_rows,
        out_shape=jax.ShapeDtypeStruct((BCAP, width), jnp.bfloat16),
        in_specs=[smem, vmem, vmem],
        out_specs=vmem,
        compiler_params=pltpu.CompilerParams(vmem_limit_bytes=24 << 20),
        name="pick_rows",
    )(me, ids, tokens)
    gathered = lax.all_gather(rows, "curve", axis=0, tiled=True)

    from_two_behind = send(tokens, [(i, i + 2) for i in everyone if i + 2 < size])
    from_two_ahead = send(tokens, [(i, i - 2) for i in everyone if i >= 2])
    mate = send(tokens, [(i, i ^ 1) for i in everyone])

    wvt, plan, qbd, *sums = run_phase(
        FIRST, [tokens], w_keyval, nbound, lists=(me, block_list, block_count), wq=w_query
    )

    after = jnp.minimum(plan[7, 0], 0)
    half = tok_dev // 2
    relay = jnp.where(member % 2 == after, from_two_ahead[:half], from_two_behind[:half])
    low = send(relay, [(i, i ^ 1) for i in everyone])
    hops = [(i, i + 2 - 4 * (i % 2)) for i in everyone]
    upper = lax.dynamic_slice_in_dim(mate, half + after, half)
    high = send(upper, [(a, b) for a, b in hops if 0 <= b < size])

    sums = run_phase(
        MIDDLE,
        [from_two_behind, from_two_ahead, mate],
        w_keyval,
        nbound,
        state=[wvt, plan, qbd, *sums],
    )
    far = jnp.concatenate([low, high], axis=0)
    (mixed,) = run_phase(
        LAST, [far], w_keyval, nbound, state=[wvt, plan, qbd, *sums], ends=(ids, gathered, w_out)
    )
    return mixed


def solution(mesh):
    in_specs = (
        P(("geo", "curve"), None),
        P(),
        P(),
        P(),
        P(("geo", "curve"), None),
        P(("geo", "curve")),
        P("geo"),
    )
    out_specs = P(("geo", "curve"), None)
    return jax.shard_map(
        on_device, mesh=mesh, in_specs=in_specs, out_specs=out_specs, check_vma=False
    )
```

time: 115 us -> 109 us (0.948)
  the two profiles are of different devices: /device:TPU:8 before, /device:TPU:10 now
where the time goes in v2:
time: 109 us; the launch traced here: 108 us
  Pallas kernels  59.9 us (55%)
  local copies, waits for them, and re-layouts  22.1 us (20%)
  between operations  14.3 us (13%)
  starting transfers between devices  12 us (11%)
    pallas_call x3, Pallas kernels, run_phase(): pl.pallas_call(functools.partial(phase, kind, len(toks), nbound), out_sha...  58.8 us
    unnamed x44, local copies, waits for them, and re-layouts  21.4 us
    ppermute x5, starting transfers between devices, send(): return lax.ppermute(value, 'curve', pairs)  12 us
  transfers between devices with their start and end apart: 6, of which 0 were waited for; matrix products, arithmetic and copies ran while one was open for 1% of the time, Pallas kernels for 33%

profile of v2, /device:TPU:10, one launch (start us, length us, event | category | flops | bytes accessed | tf_op | source)
XLA Modules:
  0.0 108.5 jit_solution(10632693858500401507)
XLA Ops:
  6.5 0.0 all-gather.2.cloned.1.call-start
  6.5 2.3 %collective-permute-start = (bf16[1024,512]{1,0:T(8,128)(2,1)}, bf16[1024,512]{1,0:T(8,128)(2,1)S(1)}, u32[]{:S(2)}, u32[]{:S(2)}) collective-permute-start(bf16[1024,512]{1,0:T(8,128)(2,1)} %tokens.1), channel_id=1, source_target_pairs={{2,0},{3,1},{4,2},{5,3},{6,4},{7,5},{10,8},{11,9},{12,10},{13,11},... | collective-permute-start | bytes 3145736 | tf_op jit(solution)/shard_map/ppermute | solution.py:331
  8.9 3.5 %collective-permute-start.1 = (bf16[1024,512]{1,0:T(8,128)(2,1)}, bf16[1024,512]{1,0:T(8,128)(2,1)S(1)}, u32[]{:S(2)}, u32[]{:S(2)}) collective-permute-start(bf16[1024,512]{1,0:T(8,128)(2,1)} %tokens.1), channel_id=1, source_target_pairs={{0,2},{1,3},{2,4},{3,5},{4,6},{5,7},{8,10},{9,11},{10,12},{11,13},... | collective-permute-start | bytes 3145736 | tf_op jit(solution)/shard_map/ppermute | solution.py:331
  12.4 1.6 %collective-permute-start.3 = (bf16[1024,512]{1,0:T(8,128)(2,1)}, bf16[1024,512]{1,0:T(8,128)(2,1)S(1)}, u32[]{:S(2)}, u32[]{:S(2)}) collective-permute-start(bf16[1024,512]{1,0:T(8,128)(2,1)} %tokens.1), channel_id=1, source_target_pairs={{0,1},{1,0},{2,3},{3,2},{4,5},{5,4},{6,7},{7,6},{8,9},{9,8},{10,11... | collective-permute-start | bytes 3145736 | tf_op jit(solution)/shard_map/ppermute | solution.py:331
  14.0 0.0 copy-start
  14.0 1.3 %copy-done = bf16[1024,512]{1,0:T(8,128)(2,1)S(1)} copy-done((bf16[1024,512]{1,0:T(8,128)(2,1)S(1)}, bf16[1024,512]{1,0:T(8,128)(2,1)}, u32[]{:S(2)}) %copy-start) | copy-done | bytes 1048600
  15.2 0.0 copy-start.2
  15.2 0.7 copy-done.2
  15.9 1.1 %pick_rows.1 = bf16[128,512]{1,0:T(8,128)(2,1)} custom-call(s32[1]{0:T(128)} %bitcast.refs_2_.me_ref, s32[1,512]{1,0:T(1,128)S(1)} %bitcast.3, bf16[1024,512]{1,0:T(8,128)(2,1)S(1)} %copy-done), custom_call_target="tpu_custom_call" | custom-call | tf_op jit(solution)/shard_map/pick_rows/pallas_call | solution.py:344
  17.0 0.0 all-gather.2.cloned.1.call-update
  17.1 0.0 copy-start.1
  17.1 1.2 %copy-done.1 = bf16[1024,512]{1,0:T(8,128)(2,1)S(1)} copy-done((bf16[1024,512]{1,0:T(8,128)(2,1)S(1)}, bf16[1024,512]{1,0:T(8,128)(2,1)}, u32[]{:S(2)}) %copy-start.1) | copy-done | bytes 1048600
  18.3 0.0 copy-start.4
  18.3 1.2 %copy-done.4 = bf16[512,1024]{1,0:T(8,128)(2,1)S(1)} copy-done((bf16[512,1024]{1,0:T(8,128)(2,1)S(1)}, bf16[512,1024]{1,0:T(8,128)(2,1)}, u32[]{:S(2)}) %copy-start.4) | copy-done | bytes 1048600
  19.5 0.0 copy-start.8
  19.5 1.0 copy-done.8
  20.6 0.0 copy-start.10
  20.6 0.7 copy-done.10
  21.2 0.0 copy-start.11
  21.3 0.7 copy-done.11
  21.9 13.6 %attend_own.1 = (bf16[512,512]{1,0:T(8,128)(2,1)S(1)}, s32[8,128]{1,0:T(8,128)S(1)}, bf16[8,4,128,256]{3,2,1,0:T(8,128)(2,1)S(1)}, f32[32,128,128]{2,1,0:T(8,128...) custom-call(bf16[1024,512]{1,0:T(8,128)(2,1)S(1)} %copy-done.1, bf16[512,1024]{1,0:T(8,128)(2,1)S(1)} %copy-done.4, ...), custom_call_target="tpu_custom_call" | custom-call | flops 5905580032 | bytes 8388608 | tf_op jit(solution)/shard_map/attend_own/pallas_call | solution.py:318
  35.5 0.0 copy-start.12
  35.5 1.3 %copy-done.12 = bf16[8,4,128,256]{3,2,1,0:T(8,128)(2,1)} copy-done((bf16[8,4,128,256]{3,2,1,0:T(8,128)(2,1)}, bf16[8,4,128,256]{3,2,1,0:T(8,128)(2,1)S(1)}, u32[]{:S(2)}) %copy-start.12) | copy-done | bytes 2097176
  36.9 0.0 copy-start.15
  36.9 1.3 %copy-done.15 = f32[32,128,128]{2,1,0:T(8,128)} copy-done((f32[32,128,128]{2,1,0:T(8,128)}, f32[32,128,128]{2,1,0:T(8,128)S(1)}, u32[]{:S(2)}) %copy-start.15) | copy-done | bytes 2097176
  38.2 0.0 copy-start.19
  38.2 0.8 copy-done.19
  39.0 0.6 slice.9
  40.3 0.0 copy-start.5
  40.3 0.0 copy-start.20
  40.3 0.0 collective-permute-done.refs_1_
  40.3 0.0 collective-permute-done.1.refs_0_
  40.3 0.1 slice_select_fusion
  40.4 1.1 %collective-permute-start.2 = (bf16[512,512]{1,0:T(8,128)(2,1)S(1)}, bf16[512,512]{1,0:T(8,128)(2,1)S(1)}, u32[]{:S(2)}, u32[]{:S(2)}) collective-permute-start(bf16[512,512]{1,0:T(8,128)(2,1)S(1)} %slice_select_fusion), channel_id=1, source_target_pairs={{0,1},{1,0},{2,3},{3,2},{4,5},{5,4},{6,7},{7,6},{8,9},{9,8},{10,11... | collective-permute-start | bytes 1572872 | tf_op jit(solution)/shard_map/ppermute | solution.py:331
  41.5 0.0 collective-permute-done.3.refs_2_
  41.5 0.1 constant_dynamic-slice_fusion
  41.6 3.5 %collective-permute-start.4 = (bf16[512,512]{1,0:T(8,128)(2,1)S(1)}, bf16[512,512]{1,0:T(8,128)(2,1)S(1)}, u32[]{:S(2)}, u32[]{:S(2)}) collective-permute-start(bf16[512,512]{1,0:T(8,128)(2,1)S(1)} %constant_dynamic-slice_fusion), channel_id=1, source_target_pairs={{0,2},{2,4},{3,1},{4,6},{5,3},{7,5},{8,10},{10,12},{11,9},{12,14},... | collective-permute-start | bytes 1572872 | tf_op jit(solution)/shard_map/ppermute | solution.py:331
  45.1 0.0 copy-done.5
  45.1 0.0 copy-done.20
  45.1 0.0 copy-start.13
  45.1 1.6 %copy-done.13 = bf16[8,4,128,256]{3,2,1,0:T(8,128)(2,1)S(1)} copy-done((bf16[8,4,128,256]{3,2,1,0:T(8,128)(2,1)S(1)}, bf16[8,4,128,256]{3,2,1,0:T(8,128)(2,1)}, u32[]{:S(2)}) %copy-start.13) | copy-done | bytes 2097176
  46.7 0.0 copy-start.16
  46.7 1.6 %copy-done.16 = f32[32,128,128]{2,1,0:T(8,128)S(1)} copy-done((f32[32,128,128]{2,1,0:T(8,128)S(1)}, f32[32,128,128]{2,1,0:T(8,128)}, u32[]{:S(2)}) %copy-start.16) | copy-done | bytes 2097176
  48.3 21.0 %attend_middle.1 = (f32[32,128,128]{2,1,0:T(8,128)S(1)}, f32[33,1,256]{2,1,0:T(1,128)S(1)}, f32[32,1,256]{2,1,0:T(1,128)S(1)}) custom-call(bf16[1024,512]{1,0:T(8,128)(2,1)S(1)} %collective-permute-done.1.refs_0_, bf16[1024,512]{1,0:T(8,128)(2,1)S(1)} %collective-permute-done.refs_1_, bf16[1024,512]{1,0:T(8,128)(2,1)S(1)} %collective-permute-done.3.refs_2_, ...), custom_call_target="tpu_custom_call" | custom-call | flops 12348030976 | bytes 8388608 | tf_op jit(solution)/shard_map/attend_middle/pallas_call | solution.py:318
  69.3 0.0 copy-start.17
  69.3 1.3 %copy-done.17 = f32[32,128,128]{2,1,0:T(8,128)} copy-done((f32[32,128,128]{2,1,0:T(8,128)}, f32[32,128,128]{2,1,0:T(8,128)S(1)}, u32[]{:S(2)}) %copy-start.17) | copy-done | bytes 2097176
  70.6 0.0 copy-start.3
  70.6 0.0 copy-start.6
  70.6 0.0 copy-start.9
  70.6 0.0 collective-permute-done.2
  70.7 0.0 collective-permute-done.4
  70.7 0.1 pad_maximum_fusion.refs_0_
  70.7 0.0 all-gather.2.cloned.1.call-done.refs_9_
  70.8 0.6 copy-done.3
  71.3 0.6 copy-done.6
  71.9 0.1 copy-done.9
  72.0 1.2 %copy-done.7 = bf16[1024,512]{1,0:T(8,128)(2,1)S(1)} copy-done((bf16[1024,512]{1,0:T(8,128)(2,1)S(1)}, bf16[1024,512]{1,0:T(8,128)(2,1)}, u32[]{:S(2)}) %copy-start.7) | copy-done | bytes 1048600
  73.2 0.0 copy-start.14
  73.2 1.6 %copy-done.14 = bf16[8,4,128,256]{3,2,1,0:T(8,128)(2,1)S(1)} copy-done((bf16[8,4,128,256]{3,2,1,0:T(8,128)(2,1)S(1)}, bf16[8,4,128,256]{3,2,1,0:T(8,128)(2,1)}, u32[]{:S(2)}) %copy-start.14) | copy-done | bytes 2097176
  74.8 0.0 copy-start.18
  74.8 1.6 %copy-done.18 = f32[32,128,128]{2,1,0:T(8,128)S(1)} copy-done((f32[32,128,128]{2,1,0:T(8,128)S(1)}, f32[32,128,128]{2,1,0:T(8,128)}, u32[]{:S(2)}) %copy-start.18) | copy-done | bytes 2097176
  76.4 0.0 copy-start.21
  76.4 1.0 copy-done.21
  77.5 24.2 %attend_last.1 = bf16[1024,512]{1,0:T(8,128)(2,1)} custom-call(bf16[1024,512]{1,0:T(8,128)(2,1)S(1)} %pad_maximum_fusion.refs_0_, bf16[512,1024]{1,0:T(8,128)(2,1)S(1)} %copy-done.6, bf16[512,512]{1,0:T(8,128)(2,1)S(1)} %copy-done.21, s32[8,128]{1,0:T(8,128)S(1)} %get-tuple-element.14.refs_5_.refs_3_, bf16[8,4,128,256]{3,2,1,0:T(8,128)(2,1)S(1)} %copy-done.14, ...), custom_call_target="tpu_custom_call" | custom-call | flops 13153337344 | bytes 8388608 | tf_op jit(solution)/shard_map/attend_last/pallas_call | solution.py:318
  (1 shorter events, 0.0 us)
Async XLA Ops:
  6.5 64.2 %all-gather.2.cloned.1.call-start = ((), (), s32[]{:S(2)}) async-start(), calls=%async_computation | async-start | bytes 1179648 | tf_op jit(solution)/shard_map/all_gather | solution.py:352
  6.5 33.8 %collective-permute-start = (bf16[1024,512]{1,0:T(8,128)(2,1)}, bf16[1024,512]{1,0:T(8,128)(2,1)S(1)}, u32[]{:S(2)}, u32[]{:S(2)}) collective-permute-start(bf16[1024,512]{1,0:T(8,128)(2,1)} %tokens.1), channel_id=1, source_target_pairs={{2,0},{3,1},{4,2},{5,3},{6,4},{7,5},{10,8},{11,9},{12,10},{13,11},... | collective-permute-start | bytes 3145736 | tf_op jit(solution)/shard_map/ppermute | solution.py:331
  8.9 31.4 %collective-permute-start.1 = (bf16[1024,512]{1,0:T(8,128)(2,1)}, bf16[1024,512]{1,0:T(8,128)(2,1)S(1)}, u32[]{:S(2)}, u32[]{:S(2)}) collective-permute-start(bf16[1024,512]{1,0:T(8,128)(2,1)} %tokens.1), channel_id=1, source_target_pairs={{0,2},{1,3},{2,4},{3,5},{4,6},{5,7},{8,10},{9,11},{10,12},{11,13},... | collective-permute-start | bytes 3145736 | tf_op jit(solution)/shard_map/ppermute | solution.py:331
  12.4 29.1 %collective-permute-start.3 = (bf16[1024,512]{1,0:T(8,128)(2,1)}, bf16[1024,512]{1,0:T(8,128)(2,1)S(1)}, u32[]{:S(2)}, u32[]{:S(2)}) collective-permute-start(bf16[1024,512]{1,0:T(8,128)(2,1)} %tokens.1), channel_id=1, source_target_pairs={{0,1},{1,0},{2,3},{3,2},{4,5},{5,4},{6,7},{7,6},{8,9},{9,8},{10,11... | collective-permute-start | bytes 3145736 | tf_op jit(solution)/shard_map/ppermute | solution.py:331
  14.0 1.3 %copy-start = (bf16[1024,512]{1,0:T(8,128)(2,1)S(1)}, bf16[1024,512]{1,0:T(8,128)(2,1)}, u32[]{:S(2)}) copy-start(bf16[1024,512]{1,0:T(8,128)(2,1)} %tokens.1) | copy-start | bytes 3145732
  15.2 0.7 copy-start.2
  17.1 1.2 %copy-start.1 = (bf16[1024,512]{1,0:T(8,128)(2,1)S(1)}, bf16[1024,512]{1,0:T(8,128)(2,1)}, u32[]{:S(2)}) copy-start(bf16[1024,512]{1,0:T(8,128)(2,1)} %tokens.1) | copy-start | bytes 3145732
  18.3 1.2 %copy-start.4 = (bf16[512,1024]{1,0:T(8,128)(2,1)S(1)}, bf16[512,1024]{1,0:T(8,128)(2,1)}, u32[]{:S(2)}) copy-start(bf16[512,1024]{1,0:T(8,128)(2,1)} %refs_1_.3) | copy-start | bytes 3145732
  19.5 1.0 copy-start.8
  20.6 0.7 copy-start.10
  21.2 0.7 copy-start.11
  35.5 1.3 %copy-start.12 = (bf16[8,4,128,256]{3,2,1,0:T(8,128)(2,1)}, bf16[8,4,128,256]{3,2,1,0:T(8,128)(2,1)S(1)}, u32[]{:S(2)}) copy-start(bf16[8,4,128,256]{3,2,1,0:T(8,128)(2,1)S(1)} %get-tuple-element.16.refs_6_.refs_4_) | copy-start | bytes 6291460
  36.9 1.3 %copy-start.15 = (f32[32,128,128]{2,1,0:T(8,128)}, f32[32,128,128]{2,1,0:T(8,128)S(1)}, u32[]{:S(2)}) copy-start(f32[32,128,128]{2,1,0:T(8,128)S(1)} %get-tuple-element.17.refs_7_) | copy-start | bytes 6291460
  38.2 0.8 copy-start.19
  40.3 4.8 %copy-start.5 = (bf16[512,1024]{1,0:T(8,128)(2,1)S(1)}, bf16[512,1024]{1,0:T(8,128)(2,1)}, u32[]{:S(2)}) copy-start(bf16[512,1024]{1,0:T(8,128)(2,1)} %refs_1_.3) | copy-start | bytes 3145732
  40.3 4.8 %copy-start.20 = (bf16[512,512]{1,0:T(8,128)(2,1)S(1)}, bf16[512,512]{1,0:T(8,128)(2,1)}, u32[]{:S(2)}) copy-start(bf16[512,512]{1,0:T(8,128)(2,1)} %copy-done.19) | copy-start | bytes 1572868
  40.4 30.3 %collective-permute-start.2 = (bf16[512,512]{1,0:T(8,128)(2,1)S(1)}, bf16[512,512]{1,0:T(8,128)(2,1)S(1)}, u32[]{:S(2)}, u32[]{:S(2)}) collective-permute-start(bf16[512,512]{1,0:T(8,128)(2,1)S(1)} %slice_select_fusion), channel_id=1, source_target_pairs={{0,1},{1,0},{2,3},{3,2},{4,5},{5,4},{6,7},{7,6},{8,9},{9,8},{10,11... | collective-permute-start | bytes 1572872 | tf_op jit(solution)/shard_map/ppermute | solution.py:331
  41.6 29.0 %collective-permute-start.4 = (bf16[512,512]{1,0:T(8,128)(2,1)S(1)}, bf16[512,512]{1,0:T(8,128)(2,1)S(1)}, u32[]{:S(2)}, u32[]{:S(2)}) collective-permute-start(bf16[512,512]{1,0:T(8,128)(2,1)S(1)} %constant_dynamic-slice_fusion), channel_id=1, source_target_pairs={{0,2},{2,4},{3,1},{4,6},{5,3},{7,5},{8,10},{10,12},{11,9},{12,14},... | collective-permute-start | bytes 1572872 | tf_op jit(solution)/shard_map/ppermute | solution.py:331
  45.1 1.6 %copy-start.13 = (bf16[8,4,128,256]{3,2,1,0:T(8,128)(2,1)S(1)}, bf16[8,4,128,256]{3,2,1,0:T(8,128)(2,1)}, u32[]{:S(2)}) copy-start(bf16[8,4,128,256]{3,2,1,0:T(8,128)(2,1)} %copy-done.12) | copy-start | bytes 6291460
  46.7 1.6 %copy-start.16 = (f32[32,128,128]{2,1,0:T(8,128)S(1)}, f32[32,128,128]{2,1,0:T(8,128)}, u32[]{:S(2)}) copy-start(f32[32,128,128]{2,1,0:T(8,128)} %copy-done.15) | copy-start | bytes 6291460
  69.3 1.3 %copy-start.17 = (f32[32,128,128]{2,1,0:T(8,128)}, f32[32,128,128]{2,1,0:T(8,128)S(1)}, u32[]{:S(2)}) copy-start(f32[32,128,128]{2,1,0:T(8,128)S(1)} %get-tuple-element.20.refs_5_) | copy-start | bytes 6291460
  70.6 0.7 copy-start.3
  70.6 1.2 %copy-start.6 = (bf16[512,1024]{1,0:T(8,128)(2,1)S(1)}, bf16[512,1024]{1,0:T(8,128)(2,1)}, u32[]{:S(2)}) copy-start(bf16[512,1024]{1,0:T(8,128)(2,1)} %refs_1_.3) | copy-start | bytes 3145732
  70.6 1.4 %copy-start.9 = (bf16[512,512]{1,0:T(8,128)(2,1)S(1)}, bf16[512,512]{1,0:T(8,128)(2,1)}, u32[]{:S(2)}) copy-start(bf16[512,512]{1,0:T(8,128)(2,1)} %refs_10_.1) | copy-start | bytes 1572868
  72.0 1.2 %copy-start.7 = (bf16[1024,512]{1,0:T(8,128)(2,1)S(1)}, bf16[1024,512]{1,0:T(8,128)(2,1)}, u32[]{:S(2)}) copy-start(bf16[1024,512]{1,0:T(8,128)(2,1)} %all-gather.2.cloned.1.call-done.refs_9_) | copy-start | bytes 3145732
  73.2 1.6 %copy-start.14 = (bf16[8,4,128,256]{3,2,1,0:T(8,128)(2,1)S(1)}, bf16[8,4,128,256]{3,2,1,0:T(8,128)(2,1)}, u32[]{:S(2)}) copy-start(bf16[8,4,128,256]{3,2,1,0:T(8,128)(2,1)} %copy-done.12) | copy-start | bytes 6291460
  74.8 1.6 %copy-start.18 = (f32[32,128,128]{2,1,0:T(8,128)S(1)}, f32[32,128,128]{2,1,0:T(8,128)}, u32[]{:S(2)}) copy-start(f32[32,128,128]{2,1,0:T(8,128)} %copy-done.17) | copy-start | bytes 6291460
  76.4 1.0 copy-start.21
Sparse Core Ops, SparseCore 0:
  17.2 46.9 all-gather.1

commit v3 on v2

--- a/solution.py
+++ b/solution.py
@@ -114,22 +114,41 @@
 def phase(kind, nsrc, nbound, *refs):
     refs = list(refs)
     take = lambda n: [refs.pop(0) for _ in range(n)]
-    toks = take(nsrc)
-    (wk,) = take(1)
-    if kind == FIRST:
-        me_ref, lists, counts, wq = take(4)
-    else:
-        wvt, plan, qbd, acc_in, m_in, l_in = take(6)
-    if kind == LAST:
-        ids, gathered, wo, out = take(4)
-    elif kind == FIRST:
-        wvt, plan, qbd = take(3)
-    acc, m_ref, l_ref, k_ref, vt_ref, p_ref, norm_ref = take(7)
+    nin = nsrc + {FIRST: 2, MIDDLE: 6, LAST: 8}[kind]
+    hbm_in = take(nin)
+    if kind == FIRST:
+        me_ref, lists, counts = take(3)
+    else:
+        (plan,) = take(1)
+    if kind == LAST:
+        ids, out = take(2)
+    else:
+        if kind == FIRST:
+            wvt_out, plan, qbd_out = take(3)
+        acc_out, m_out, l_out = take(3)
+    bufs = take(nin)
+    loads = []
+    in_sem, out_sem = refs[-2:]
+    for i in range(nin):
+        loads.append(pltpu.make_async_copy(hbm_in[i], bufs[i], in_sem.at[i]))
+        loads[i].start()
+    wk, toks = bufs[0], bufs[2:2 + nsrc]
+    if kind == FIRST:
+        wq = bufs[1]
+        wvt, qbd, acc, m_ref, l_ref = take(5)
+    else:
+        wvt, qbd = bufs[1], bufs[2 + nsrc]
+        acc, m_ref, l_ref = bufs[3 + nsrc:6 + nsrc]
+        if kind == LAST:
+            gathered, wo = bufs[6 + nsrc:8 + nsrc]
+    k_ref, vt_ref, p_ref, norm_ref = take(4)
     nqb, pairs = qbd.shape[0], qbd.shape[1]
 
     norm_ref[...] = jnp.zeros_like(norm_ref)
     if kind == FIRST:
         qn_ref, wqt = take(2)
+        for load in loads:
+            load.wait()
         wqt[...] = wq[...].T
         wvt[...] = wk[:, wvt.shape[0]:].T
         qn_ref[...] = jnp.zeros_like(qn_ref)
@@ -160,19 +179,23 @@
         l_ref[...] = jnp.zeros_like(l_ref)
         qn = jnp.max(qn_ref[...])
     else:
-        acc[...] = acc_in[...]
-        l_ref[...] = l_in[...]
-        m_ref[...] = m_in[...]
-        qn = jnp.max(m_in[nqb * pairs])
+        loads[0].wait()
+        loads[1].wait()
 
     base = 0
+    for i, tok in enumerate(toks):
+        if kind != FIRST:
+            loads[2 + i].wait()
+        project(tok, wk, wvt, k_ref, vt_ref, norm_ref, base)
+        base += tok.shape[0] // BLOCK
+    if kind != FIRST:
+        for load in loads[2 + nsrc:]:
+            load.wait()
+        qn = jnp.max(m_ref[nqb * pairs])
     if kind == LAST:
         (bound,) = take(1)
         join_rows(ids, gathered, bound, toks[0].shape[0])
-        toks = toks + [bound]
-    for tok in toks:
-        project(tok, wk, wvt, k_ref, vt_ref, norm_ref, base)
-        base += tok.shape[0] // BLOCK
+        project(bound, wk, wvt, k_ref, vt_ref, norm_ref, base)
     fast = jnp.logical_and(qn < 1e20, qn * jnp.max(norm_ref[...]) <= 3600.0)
     if kind == FIRST:
         m_ref[...] = jnp.full_like(m_ref, jnp.where(fast, 0.0, LOW))
@@ -253,6 +276,16 @@
 
         lax.fori_loop(0, 2 * count, one, 0)
 
+    if kind != LAST:
+        stores = [(acc, acc_out), (m_ref, m_out), (l_ref, l_out)]
+        if kind == FIRST:
+            stores += [(wvt, wvt_out), (qbd, qbd_out)]
+        stores = [pltpu.make_async_copy(x, y, out_sem.at[i]) for i, (x, y) in enumerate(stores)]
+        for store in stores:
+            store.start()
+        for store in stores:
+            store.wait()
+
     if kind == LAST:
         @pl.loop(0, nqb)
         def _(qb):
@@ -271,34 +304,41 @@
     pairs = width // BLOCK
     nkb = sum(t.shape[0] for t in toks) // BLOCK + (nbound // BLOCK if kind == LAST else 0)
     vmem, smem = pl.BlockSpec(memory_space=pltpu.VMEM), pl.BlockSpec(memory_space=pltpu.SMEM)
-    args, specs = list(toks) + [wk], [vmem] * (len(toks) + 1)
-    if kind == FIRST:
-        args += list(lists) + [wq]
-        specs += [smem] * 3 + [vmem]
+    hbm = pl.BlockSpec(memory_space=pltpu.HBM)
+    if kind == FIRST:
+        big, small = [wk, wq, *toks], list(lists)
+        small_specs = [smem] * 3
         nqb = toks[0].shape[0] // BLOCK
     else:
-        args += list(state)
-        specs += [vmem, smem] + [vmem] * 4
-        nqb = state[2].shape[0]
-    if kind == LAST:
-        args += list(ends)
-        specs += [vmem] * 3
-    sums = [(nqb * pairs, BLOCK, BLOCK), (nqb * pairs + 1, 1, 2 * BLOCK), (nqb * pairs, 1, 2 * BLOCK)]
-    outs, out_specs, scratch = [], [], []
+        wvt, plan, qbd, *sums = state
+        big, small = [wk, wvt, *toks, qbd, *sums], [plan]
+        small_specs = [smem]
+        nqb = qbd.shape[0]
+    if kind == LAST:
+        ids, gathered, wo = ends
+        big += [gathered, wo]
+        small.append(ids)
+        small_specs.append(vmem)
+    args, specs = big + small, [hbm] * len(big) + small_specs
+    shapes = [(nqb * pairs, BLOCK, BLOCK), (nqb * pairs + 1, 1, 2 * BLOCK), (nqb * pairs, 1, 2 * BLOCK)]
+    q_shape = (nqb, pairs, BLOCK, 2 * BLOCK)
+    outs, out_specs = [], []
+    scratch = [pltpu.VMEM(x.shape, x.dtype) for x in big]
     if kind == LAST:
         outs.append(jax.ShapeDtypeStruct((nqb * BLOCK, width), jnp.bfloat16))
         out_specs.append(vmem)
-        scratch += [pltpu.VMEM(s, jnp.float32) for s in sums]
     else:
         if kind == FIRST:
             outs += [
                 jax.ShapeDtypeStruct((width, width), jnp.bfloat16),
                 jax.ShapeDtypeStruct((8, PLAN_LEN), jnp.int32),
-                jax.ShapeDtypeStruct((nqb, pairs, BLOCK, 2 * BLOCK), jnp.bfloat16),
+                jax.ShapeDtypeStruct(q_shape, jnp.bfloat16),
             ]
-            out_specs += [vmem, smem, vmem]
-        outs += [jax.ShapeDtypeStruct(s, jnp.float32) for s in sums]
-        out_specs += [vmem] * 3
+            out_specs += [hbm, smem, hbm]
+            scratch += [pltpu.VMEM((width, width), jnp.bfloat16), pltpu.VMEM(q_shape, jnp.bfloat16)]
+            scratch += [pltpu.VMEM(s, jnp.float32) for s in shapes]
+        outs += [jax.ShapeDtypeStruct(s, jnp.float32) for s in shapes]
+        out_specs += [hbm] * 3
     scratch += [
         pltpu.VMEM((nkb, BLOCK, width), jnp.bfloat16),
         pltpu.VMEM((nkb, width, BLOCK), jnp.bfloat16),
@@ -309,6 +349,7 @@
         scratch += [pltpu.VMEM((1, ROWS), jnp.float32), pltpu.VMEM((width, width), jnp.bfloat16)]
     if kind == LAST:
         scratch.append(pltpu.VMEM((nbound, width), jnp.bfloat16))
+    scratch += [pltpu.SemaphoreType.DMA((len(big),)), pltpu.SemaphoreType.DMA((5,))]
     units = {FIRST: 18, MIDDLE: 34, LAST: 43}[kind]
     cost = pl.CostEstimate(
         flops=units * 8 * 2 * BLOCK ** 3 * 8 + nkb * BLOCK * width * width * 4,
@@ -321,7 +362,7 @@
         in_specs=specs,
         out_specs=out_specs,
         scratch_shapes=scratch,
-        compiler_params=pltpu.CompilerParams(vmem_limit_bytes=24 << 20),
+        compiler_params=pltpu.CompilerParams(vmem_limit_bytes=63 << 20),
         cost_estimate=cost,
         name=("attend_own", "attend_middle", "attend_last")[kind],
     )(*args)
@@ -346,7 +387,7 @@
         out_shape=jax.ShapeDtypeStruct((BCAP, width), jnp.bfloat16),
         in_specs=[smem, vmem, vmem],
         out_specs=vmem,
-        compiler_params=pltpu.CompilerParams(vmem_limit_bytes=24 << 20),
+        compiler_params=pltpu.CompilerParams(vmem_limit_bytes=63 << 20),
         name="pick_rows",
     )(me, ids, tokens)
     gathered = lax.all_gather(rows, "curve", axis=0, tiled=True)

time: 109 us -> 108 us (level)
  the two profiles are of different devices: /device:TPU:10 before, /device:TPU:18 now
where the time goes in v3:
time: 108 us
  Pallas kernels  67.5 us (62%)
  starting transfers between devices  14.3 us (13%)
  between operations  14.1 us (13%)
  waiting for transfers between devices  5.71 us (5%)
  other arithmetic  3.49 us (3%)
  local copies, waits for them, and re-layouts  3.16 us (3%)
    pallas_call x3, Pallas kernels, run_phase(): pl.pallas_call(functools.partial(phase, kind, len(toks), nbound), out_sha...  65.1 us
    ppermute x5, starting transfers between devices, send(): return lax.ppermute(value, 'curve', pairs)  14.3 us
    ppermute x5, waiting for transfers between devices, send(): return lax.ppermute(value, 'curve', pairs)  5.69 us
    pallas_call x1, Pallas kernels, on_device(): pl.pallas_call(pick_rows, out_shape=jax.ShapeDtypeStruct((BCAP, width), j...  2.39 us
    concatenate x1, other arithmetic, on_device(): far = jnp.concatenate([low, high], axis=0)  2.23 us
  transfers between devices with their start and end apart: 6, of which 2 were waited for; matrix products, arithmetic and copies ran while one was open for 6% of the time, Pallas kernels for 37%

profile of v3, /device:TPU:18, one launch (start us, length us, event | category | flops | bytes accessed | tf_op | source)
XLA Modules:
  0.0 108.3 jit_solution(9832117052715071631)
XLA Ops:
  6.5 0.0 all-gather.2.cloned.1.call-start
  6.5 2.3 %collective-permute-start = (bf16[1024,512]{1,0:T(8,128)(2,1)}, bf16[1024,512]{1,0:T(8,128)(2,1)}, u32[]{:S(2)}, u32[]{:S(2)}) collective-permute-start(bf16[1024,512]{1,0:T(8,128)(2,1)} %tokens.1), channel_id=1, source_target_pairs={{2,0},{3,1},{4,2},{5,3},{6,4},{7,5},{10,8},{11,9},{12,10},{13,11},... | collective-permute-start | bytes 3145736 | tf_op jit(solution)/shard_map/ppermute | solution.py:372
  8.9 4.4 %collective-permute-start.1 = (bf16[1024,512]{1,0:T(8,128)(2,1)}, bf16[1024,512]{1,0:T(8,128)(2,1)}, u32[]{:S(2)}, u32[]{:S(2)}) collective-permute-start(bf16[1024,512]{1,0:T(8,128)(2,1)} %tokens.1), channel_id=1, source_target_pairs={{0,2},{1,3},{2,4},{3,5},{4,6},{5,7},{8,10},{9,11},{10,12},{11,13},... | collective-permute-start | bytes 3145736 | tf_op jit(solution)/shard_map/ppermute | solution.py:372
  13.3 1.6 %collective-permute-start.3 = (bf16[1024,512]{1,0:T(8,128)(2,1)}, bf16[1024,512]{1,0:T(8,128)(2,1)}, u32[]{:S(2)}, u32[]{:S(2)}) collective-permute-start(bf16[1024,512]{1,0:T(8,128)(2,1)} %tokens.1), channel_id=1, source_target_pairs={{0,1},{1,0},{2,3},{3,2},{4,5},{5,4},{6,7},{7,6},{8,9},{9,8},{10,11... | collective-permute-start | bytes 3145736 | tf_op jit(solution)/shard_map/ppermute | solution.py:372
  14.9 2.4 %pick_rows.1 = bf16[128,512]{1,0:T(8,128)(2,1)} custom-call(s32[1]{0:T(128)} %bitcast.refs_3_.me_ref, s32[1,512]{1,0:T(1,128)} %bitcast.3, bf16[1024,512]{1,0:T(8,128)(2,1)} %tokens.1), custom_call_target="tpu_custom_call" | custom-call | tf_op jit(solution)/shard_map/pick_rows/pallas_call | solution.py:385
  17.3 0.0 all-gather.2.cloned.1.call-update
  17.3 15.1 %attend_own.1 = (bf16[512,512]{1,0:T(8,128)(2,1)}, s32[8,128]{1,0:T(8,128)}, bf16[8,4,128,256]{3,2,1,0:T(8,128)(2,1)}, f32[32,128,128]{2,1,0:T(8,128)}, f32[33,1,256]{2,1,0:T(1,128)}, /*index=5*/f32[32,1,256]{2,1,0:T(1,128)}) custom-call(bf16[512,1024]{1,0:T(8,128)(2,1)} %refs_0_.5, bf16[512,512]{1,0:T(8,128)(2,1)} %refs_1_.1, bf16[1024,512]{1,0:T(8,128)(2,1)} %tokens.1, ...), custom_call_target="tpu_custom_call" | custom-call | flops 5905580032 | bytes 8388608 | tf_op jit(solution)/shard_map/attend_own/pallas_call | solution.py:359
  32.4 1.2 %slice.9 = s32[1,1]{1,0:T(1,128)} slice(s32[8,128]{1,0:T(8,128)} %get-tuple-element.15.refs_9_), slice={[7:8], [0:1]} | slice | bytes 8 | tf_op jit(solution)/shard_map/slice | solution.py:403
  34.3 3.6 %collective-permute-done.refs_3_ = bf16[1024,512]{1,0:T(8,128)(2,1)} collective-permute-done((bf16[1024,512]{1,0:T(8,128)(2,1)}, bf16[1024,512]{1,0:T(8,128)(2,1)}, u32[]{:S(2)}, u32[]{:S(2)}) %collective-permute-start) | collective-permute-done | bytes 1048608 | tf_op jit(solution)/shard_map/ppermute | solution.py:372
  37.9 2.1 %collective-permute-done.1.refs_2_ = bf16[1024,512]{1,0:T(8,128)(2,1)} collective-permute-done((bf16[1024,512]{1,0:T(8,128)(2,1)}, bf16[1024,512]{1,0:T(8,128)(2,1)}, u32[]{:S(2)}, u32[]{:S(2)}) %collective-permute-start.1) | collective-permute-done | bytes 1048608 | tf_op jit(solution)/shard_map/ppermute | solution.py:372
  40.0 1.3 %slice_select_fusion = bf16[512,512]{1,0:T(8,128)(2,1)S(1)} fusion(bf16[1024,512]{1,0:T(8,128)(2,1)} %collective-permute-done.1.refs_2_, bf16[1024,512]{1,0:T(8,128)(2,1)} %collective-permute-done.refs_3_, pred[]{:T(512)S(6)} %eq.5), kind=kLoop, calls=%fused_computation.1 | loop fusion | flops 262144 | bytes 1572865 | tf_op jit(solution)/shard_map/jit(_where)/select_n | solution.py:405
  41.2 1.6 %collective-permute-start.2 = (bf16[512,512]{1,0:T(8,128)(2,1)S(1)}, bf16[512,512]{1,0:T(8,128)(2,1)}, u32[]{:S(2)}, u32[]{:S(2)}) collective-permute-start(bf16[512,512]{1,0:T(8,128)(2,1)S(1)} %slice_select_fusion), channel_id=1, source_target_pairs={{0,1},{1,0},{2,3},{3,2},{4,5},{5,4},{6,7},{7,6},{8,9},{9,8},{10,11... | collective-permute-start | bytes 1572872 | tf_op jit(solution)/shard_map/ppermute | solution.py:372
  42.8 0.0 collective-permute-done.3.refs_4_
  42.8 2.0 %constant_dynamic-slice_fusion = bf16[512,512]{1,0:T(8,128)(2,1)} fusion(bf16[1024,512]{1,0:T(8,128)(2,1)} %collective-permute-done.3.refs_4_, s32[]{:T(128)S(6)} %select_n.21), kind=kLoop, calls=%fused_computation.2 | loop fusion | bytes 1048580 | tf_op jit(solution)/shard_map/dynamic_slice | solution.py:408
  44.8 4.4 %collective-permute-start.4 = (bf16[512,512]{1,0:T(8,128)(2,1)}, bf16[512,512]{1,0:T(8,128)(2,1)}, u32[]{:S(2)}, u32[]{:S(2)}) collective-permute-start(bf16[512,512]{1,0:T(8,128)(2,1)} %constant_dynamic-slice_fusion), channel_id=1, source_target_pairs={{0,2},{2,4},{3,1},{4,6},{5,3},{7,5},{8,10},{10,12},{11,9},{12,14},... | collective-permute-start | bytes 1572872 | tf_op jit(solution)/shard_map/ppermute | solution.py:372
  49.2 22.7 %attend_middle.1 = (f32[32,128,128]{2,1,0:T(8,128)}, f32[33,1,256]{2,1,0:T(1,128)}, f32[32,1,256]{2,1,0:T(1,128)}) custom-call(bf16[512,1024]{1,0:T(8,128)(2,1)} %refs_0_.5, bf16[512,512]{1,0:T(8,128)(2,1)} %get-tuple-element.14.refs_1_, bf16[1024,512]{1,0:T(8,128)(2,1)} %collective-permute-done.1.refs_2_, bf16[1024,512]{1,0:T(8,128)(2,1)} %collective-permute-done.refs_3_, ...), custom_call_target="tpu_custom_call" | custom-call | flops 12348030976 | bytes 8388608 | tf_op jit(solution)/shard_map/attend_middle/pallas_call | solution.py:359
  71.9 0.0 collective-permute-done.2
  71.9 0.0 collective-permute-done.4
  71.9 2.2 %pad_maximum_fusion.refs_2_ = bf16[1024,512]{1,0:T(8,128)(2,1)} fusion(bf16[512,512]{1,0:T(8,128)(2,1)} %collective-permute-done.4, bf16[512,512]{1,0:T(8,128)(2,1)} %collective-permute-done.2), kind=kLoop, calls=%fused_computation | loop fusion | flops 2097152 | bytes 2097152 | tf_op jit(solution)/shard_map/concatenate | solution.py:418
  74.2 0.0 all-gather.2.cloned.1.call-done.refs_7_
  74.2 27.2 %attend_last.1 = bf16[1024,512]{1,0:T(8,128)(2,1)} custom-call(bf16[512,1024]{1,0:T(8,128)(2,1)} %refs_0_.5, bf16[512,512]{1,0:T(8,128)(2,1)} %get-tuple-element.14.refs_1_, bf16[1024,512]{1,0:T(8,128)(2,1)} %pad_maximum_fusion.refs_2_, bf16[8,4,128,256]{3,2,1,0:T(8,128)(2,1)} %get-tuple-element.16.refs_5_.refs_3_, ...), custom_call_target="tpu_custom_call" | custom-call | flops 13153337344 | bytes 8388608 | tf_op jit(solution)/shard_map/attend_last/pallas_call | solution.py:359
Async XLA Ops:
  6.5 67.6 %all-gather.2.cloned.1.call-start = ((), (), s32[]{:S(2)}) async-start(), calls=%async_computation | async-start | bytes 1179648 | tf_op jit(solution)/shard_map/all_gather | solution.py:393
  6.5 31.3 %collective-permute-start = (bf16[1024,512]{1,0:T(8,128)(2,1)}, bf16[1024,512]{1,0:T(8,128)(2,1)}, u32[]{:S(2)}, u32[]{:S(2)}) collective-permute-start(bf16[1024,512]{1,0:T(8,128)(2,1)} %tokens.1), channel_id=1, source_target_pairs={{2,0},{3,1},{4,2},{5,3},{6,4},{7,5},{10,8},{11,9},{12,10},{13,11},... | collective-permute-start | bytes 3145736 | tf_op jit(solution)/shard_map/ppermute | solution.py:372
  8.9 31.1 %collective-permute-start.1 = (bf16[1024,512]{1,0:T(8,128)(2,1)}, bf16[1024,512]{1,0:T(8,128)(2,1)}, u32[]{:S(2)}, u32[]{:S(2)}) collective-permute-start(bf16[1024,512]{1,0:T(8,128)(2,1)} %tokens.1), channel_id=1, source_target_pairs={{0,2},{1,3},{2,4},{3,5},{4,6},{5,7},{8,10},{9,11},{10,12},{11,13},... | collective-permute-start | bytes 3145736 | tf_op jit(solution)/shard_map/ppermute | solution.py:372
  13.3 29.5 %collective-permute-start.3 = (bf16[1024,512]{1,0:T(8,128)(2,1)}, bf16[1024,512]{1,0:T(8,128)(2,1)}, u32[]{:S(2)}, u32[]{:S(2)}) collective-permute-start(bf16[1024,512]{1,0:T(8,128)(2,1)} %tokens.1), channel_id=1, source_target_pairs={{0,1},{1,0},{2,3},{3,2},{4,5},{5,4},{6,7},{7,6},{8,9},{9,8},{10,11... | collective-permute-start | bytes 3145736 | tf_op jit(solution)/shard_map/ppermute | solution.py:372
  41.2 30.7 %collective-permute-start.2 = (bf16[512,512]{1,0:T(8,128)(2,1)S(1)}, bf16[512,512]{1,0:T(8,128)(2,1)}, u32[]{:S(2)}, u32[]{:S(2)}) collective-permute-start(bf16[512,512]{1,0:T(8,128)(2,1)S(1)} %slice_select_fusion), channel_id=1, source_target_pairs={{0,1},{1,0},{2,3},{3,2},{4,5},{5,4},{6,7},{7,6},{8,9},{9,8},{10,11... | collective-permute-start | bytes 1572872 | tf_op jit(solution)/shard_map/ppermute | solution.py:372
  44.8 27.1 %collective-permute-start.4 = (bf16[512,512]{1,0:T(8,128)(2,1)}, bf16[512,512]{1,0:T(8,128)(2,1)}, u32[]{:S(2)}, u32[]{:S(2)}) collective-permute-start(bf16[512,512]{1,0:T(8,128)(2,1)} %constant_dynamic-slice_fusion), channel_id=1, source_target_pairs={{0,2},{2,4},{3,1},{4,6},{5,3},{7,5},{8,10},{10,12},{11,9},{12,14},... | collective-permute-start | bytes 1572872 | tf_op jit(solution)/shard_map/ppermute | solution.py:372
Sparse Core Ops, SparseCore 0:
  17.5 45.5 all-gather.1

commit v4 on v3

--- a/solution.py
+++ b/solution.py
@@ -124,7 +124,7 @@
         ids, out = take(2)
     else:
         if kind == FIRST:
-            wvt_out, plan, qbd_out = take(3)
+            wvt_out, plan, qbd_out, tok_out = take(4)
         acc_out, m_out, l_out = take(3)
     bufs = take(nin)
     loads = []
@@ -132,6 +132,9 @@
     for i in range(nin):
         loads.append(pltpu.make_async_copy(hbm_in[i], bufs[i], in_sem.at[i]))
         loads[i].start()
+    if kind == FIRST:
+        again = pltpu.make_async_copy(hbm_in[2], tok_out, out_sem.at[5])
+        again.start()
     wk, toks = bufs[0], bufs[2:2 + nsrc]
     if kind == FIRST:
         wq = bufs[1]
@@ -285,6 +288,8 @@
             store.start()
         for store in stores:
             store.wait()
+        if kind == FIRST:
+            again.wait()
 
     if kind == LAST:
         @pl.loop(0, nqb)
@@ -333,8 +338,9 @@
                 jax.ShapeDtypeStruct((width, width), jnp.bfloat16),
                 jax.ShapeDtypeStruct((8, PLAN_LEN), jnp.int32),
                 jax.ShapeDtypeStruct(q_shape, jnp.bfloat16),
+                jax.ShapeDtypeStruct(toks[0].shape, jnp.bfloat16),
             ]
-            out_specs += [hbm, smem, hbm]
+            out_specs += [hbm, smem, hbm, hbm]
             scratch += [pltpu.VMEM((width, width), jnp.bfloat16), pltpu.VMEM(q_shape, jnp.bfloat16)]
             scratch += [pltpu.VMEM(s, jnp.float32) for s in shapes]
         outs += [jax.ShapeDtypeStruct(s, jnp.float32) for s in shapes]
@@ -349,7 +355,7 @@
         scratch += [pltpu.VMEM((1, ROWS), jnp.float32), pltpu.VMEM((width, width), jnp.bfloat16)]
     if kind == LAST:
         scratch.append(pltpu.VMEM((nbound, width), jnp.bfloat16))
-    scratch += [pltpu.SemaphoreType.DMA((len(big),)), pltpu.SemaphoreType.DMA((5,))]
+    scratch += [pltpu.SemaphoreType.DMA((len(big),)), pltpu.SemaphoreType.DMA((6,))]
     units = {FIRST: 18, MIDDLE: 34, LAST: 43}[kind]
     cost = pl.CostEstimate(
         flops=units * 8 * 2 * BLOCK ** 3 * 8 + nkb * BLOCK * width * width * 4,
@@ -396,17 +402,12 @@
     from_two_ahead = send(tokens, [(i, i - 2) for i in everyone if i >= 2])
     mate = send(tokens, [(i, i ^ 1) for i in everyone])
 
-    wvt, plan, qbd, *sums = run_phase(
+    wvt, plan, qbd, again, *sums = run_phase(
         FIRST, [tokens], w_keyval, nbound, lists=(me, block_list, block_count), wq=w_query
     )
 
-    after = jnp.minimum(plan[7, 0], 0)
-    half = tok_dev // 2
-    relay = jnp.where(member % 2 == after, from_two_ahead[:half], from_two_behind[:half])
-    low = send(relay, [(i, i ^ 1) for i in everyone])
-    hops = [(i, i + 2 - 4 * (i % 2)) for i in everyone]
-    upper = lax.dynamic_slice_in_dim(mate, half + after, half)
-    high = send(upper, [(a, b) for a, b in hops if 0 <= b < size])
+    hops = [(i, i + 1 if i % 2 else i - 1) for i in everyone]
+    far = send(again, [(a, b) for a, b in hops if 0 <= b < size])
 
     sums = run_phase(
         MIDDLE,
@@ -415,7 +416,6 @@
         nbound,
         state=[wvt, plan, qbd, *sums],
     )
-    far = jnp.concatenate([low, high], axis=0)
     (mixed,) = run_phase(
         LAST, [far], w_keyval, nbound, state=[wvt, plan, qbd, *sums], ends=(ids, gathered, w_out)
     )

time: 108 us -> 114 us (1.056)
  the two profiles are of different devices: /device:TPU:18 before, /device:TPU:15 now
where the time goes in v4:
time: 114 us; the launch traced here: 111 us
  Pallas kernels  81.7 us (72%)
  between operations  13.5 us (12%)
  starting transfers between devices  9.74 us (9%)
  waiting for transfers between devices  6.6 us (6%)
    pallas_call x3, Pallas kernels, run_phase(): pl.pallas_call(functools.partial(phase, kind, len(toks), nbound), out_sha...  79.3 us
    ppermute x4, starting transfers between devices, send(): return lax.ppermute(value, 'curve', pairs)  9.73 us
    ppermute x4, waiting for transfers between devices, send(): return lax.ppermute(value, 'curve', pairs)  6.58 us
    pallas_call x1, Pallas kernels, on_device(): pl.pallas_call(pick_rows, out_shape=jax.ShapeDtypeStruct((BCAP, width), j...  2.39 us
  transfers between devices with their start and end apart: 5, of which 1 were waited for; matrix products, arithmetic and copies ran while one was open for 0% of the time, Pallas kernels for 51%

profile of v4, /device:TPU:15, one launch (start us, length us, event | category | flops | bytes accessed | tf_op | source)
XLA Modules:
  0.0 111.5 jit_solution(17350073026575958440)
XLA Ops:
  6.5 0.0 all-gather.2.cloned.1.call-start
  6.5 3.2 %collective-permute-start.1 = (bf16[1024,512]{1,0:T(8,128)(2,1)}, bf16[1024,512]{1,0:T(8,128)(2,1)}, u32[]{:S(2)}, u32[]{:S(2)}) collective-permute-start(bf16[1024,512]{1,0:T(8,128)(2,1)} %tokens.1), channel_id=1, source_target_pairs={{0,2},{1,3},{2,4},{3,5},{4,6},{5,7},{8,10},{9,11},{10,12},{11,13},... | collective-permute-start | bytes 3145736 | tf_op jit(solution)/shard_map/ppermute | solution.py:378
  9.7 3.1 %collective-permute-start.2 = (bf16[1024,512]{1,0:T(8,128)(2,1)}, bf16[1024,512]{1,0:T(8,128)(2,1)}, u32[]{:S(2)}, u32[]{:S(2)}) collective-permute-start(bf16[1024,512]{1,0:T(8,128)(2,1)} %tokens.1), channel_id=1, source_target_pairs={{2,0},{3,1},{4,2},{5,3},{6,4},{7,5},{10,8},{11,9},{12,10},{13,11},... | collective-permute-start | bytes 3145736 | tf_op jit(solution)/shard_map/ppermute | solution.py:378
  12.8 0.3 collective-permute-start.3
  13.1 2.4 %pick_rows.1 = bf16[128,512]{1,0:T(8,128)(2,1)} custom-call(s32[1]{0:T(128)} %bitcast.refs_3_.me_ref, s32[1,512]{1,0:T(1,128)} %bitcast.2, bf16[1024,512]{1,0:T(8,128)(2,1)} %tokens.1), custom_call_target="tpu_custom_call" | custom-call | tf_op jit(solution)/shard_map/pick_rows/pallas_call | solution.py:391
  15.5 0.0 all-gather.2.cloned.1.call-update
  15.5 34.3 %attend_own.1 = (bf16[512,512]{1,0:T(8,128)(2,1)}, s32[8,128]{1,0:T(8,128)}, bf16[8,4,128,256]{3,2,1,0:T(8,128)(2,1)}, bf16[1024,512]{1,0:T(8,128)(2,1)}, f32[32...) custom-call(bf16[512,1024]{1,0:T(8,128)(2,1)} %refs_0_.5, bf16[512,512]{1,0:T(8,128)(2,1)} %refs_1_.1, ...), custom_call_target="tpu_custom_call" | custom-call | flops 5905580032 | bytes 8388608 | tf_op jit(solution)/shard_map/attend_own/pallas_call | solution.py:365
  49.8 3.2 %collective-permute-start = (bf16[1024,512]{1,0:T(8,128)(2,1)}, bf16[1024,512]{1,0:T(8,128)(2,1)}, u32[]{:S(2)}, u32[]{:S(2)}) collective-permute-start(bf16[1024,512]{1,0:T(8,128)(2,1)} %get-tuple-element.16), channel_id=1, source_target_pairs={{1,2},{2,1},{3,4},{4,3},{5,6},{6,5},{9,10},{10,9},{11,12},{12,11},... | collective-permute-start | bytes 3145736 | tf_op jit(solution)/shard_map/ppermute | solution.py:378
  53.0 0.0 collective-permute-done.1.refs_2_
  53.0 0.0 collective-permute-done.2.refs_3_
  53.0 0.0 collective-permute-done.3.refs_4_
  53.0 20.3 %attend_middle.1 = (f32[32,128,128]{2,1,0:T(8,128)}, f32[33,1,256]{2,1,0:T(1,128)}, f32[32,1,256]{2,1,0:T(1,128)}) custom-call(bf16[512,1024]{1,0:T(8,128)(2,1)} %refs_0_.5, bf16[512,512]{1,0:T(8,128)(2,1)} %get-tuple-element.15.refs_1_, bf16[1024,512]{1,0:T(8,128)(2,1)} %collective-permute-done.1.refs_2_, bf16[1024,512]{1,0:T(8,128)(2,1)} %collective-permute-done.2.refs_3_, ...), custom_call_target="tpu_custom_call" | custom-call | flops 12348030976 | bytes 8388608 | tf_op jit(solution)/shard_map/attend_middle/pallas_call | solution.py:365
  73.3 6.6 %collective-permute-done.refs_2_ = bf16[1024,512]{1,0:T(8,128)(2,1)} collective-permute-done((bf16[1024,512]{1,0:T(8,128)(2,1)}, bf16[1024,512]{1,0:T(8,128)(2,1)}, u32[]{:S(2)}, u32[]{:S(2)}) %collective-permute-start) | collective-permute-done | bytes 1048608 | tf_op jit(solution)/shard_map/ppermute | solution.py:378
  79.9 0.0 all-gather.2.cloned.1.call-done.refs_7_
  79.9 24.8 %attend_last.1 = bf16[1024,512]{1,0:T(8,128)(2,1)} custom-call(bf16[512,1024]{1,0:T(8,128)(2,1)} %refs_0_.5, bf16[512,512]{1,0:T(8,128)(2,1)} %get-tuple-element.15.refs_1_, bf16[1024,512]{1,0:T(8,128)(2,1)} %collective-permute-done.refs_2_, bf16[8,4,128,256]{3,2,1,0:T(8,128)(2,1)} %get-tuple-element.17.refs_5_.refs_3_, ...), custom_call_target="tpu_custom_call" | custom-call | flops 13153337344 | bytes 8388608 | tf_op jit(solution)/shard_map/attend_last/pallas_call | solution.py:365
Async XLA Ops:
  6.5 73.3 %all-gather.2.cloned.1.call-start = ((), (), s32[]{:S(2)}) async-start(), calls=%async_computation | async-start | bytes 1179648 | tf_op jit(solution)/shard_map/all_gather | solution.py:399
  6.5 46.5 %collective-permute-start.1 = (bf16[1024,512]{1,0:T(8,128)(2,1)}, bf16[1024,512]{1,0:T(8,128)(2,1)}, u32[]{:S(2)}, u32[]{:S(2)}) collective-permute-start(bf16[1024,512]{1,0:T(8,128)(2,1)} %tokens.1), channel_id=1, source_target_pairs={{0,2},{1,3},{2,4},{3,5},{4,6},{5,7},{8,10},{9,11},{10,12},{11,13},... | collective-permute-start | bytes 3145736 | tf_op jit(solution)/shard_map/ppermute | solution.py:378
  9.7 43.3 %collective-permute-start.2 = (bf16[1024,512]{1,0:T(8,128)(2,1)}, bf16[1024,512]{1,0:T(8,128)(2,1)}, u32[]{:S(2)}, u32[]{:S(2)}) collective-permute-start(bf16[1024,512]{1,0:T(8,128)(2,1)} %tokens.1), channel_id=1, source_target_pairs={{2,0},{3,1},{4,2},{5,3},{6,4},{7,5},{10,8},{11,9},{12,10},{13,11},... | collective-permute-start | bytes 3145736 | tf_op jit(solution)/shard_map/ppermute | solution.py:378
  12.8 40.2 %collective-permute-start.3 = (bf16[1024,512]{1,0:T(8,128)(2,1)}, bf16[1024,512]{1,0:T(8,128)(2,1)}, u32[]{:S(2)}, u32[]{:S(2)}) collective-permute-start(bf16[1024,512]{1,0:T(8,128)(2,1)} %tokens.1), channel_id=1, source_target_pairs={{0,1},{1,0},{2,3},{3,2},{4,5},{5,4},{6,7},{7,6},{8,9},{9,8},{10,11... | collective-permute-start | bytes 3145736 | tf_op jit(solution)/shard_map/ppermute | solution.py:378
  49.8 30.0 %collective-permute-start = (bf16[1024,512]{1,0:T(8,128)(2,1)}, bf16[1024,512]{1,0:T(8,128)(2,1)}, u32[]{:S(2)}, u32[]{:S(2)}) collective-permute-start(bf16[1024,512]{1,0:T(8,128)(2,1)} %get-tuple-element.16), channel_id=1, source_target_pairs={{1,2},{2,1},{3,4},{4,3},{5,6},{6,5},{9,10},{10,9},{11,12},{12,11},... | collective-permute-start | bytes 3145736 | tf_op jit(solution)/shard_map/ppermute | solution.py:378
Sparse Core Ops, SparseCore 0:
  15.7 41.3 all-gather.1

commit v5 on v4

--- a/solution.py
+++ b/solution.py
@@ -117,7 +117,7 @@
     nin = nsrc + {FIRST: 2, MIDDLE: 6, LAST: 8}[kind]
     hbm_in = take(nin)
     if kind == FIRST:
-        me_ref, lists, counts = take(3)
+        me_ref, lists, counts, _ = take(4)
     else:
         (plan,) = take(1)
     if kind == LAST:
@@ -132,9 +132,6 @@
     for i in range(nin):
         loads.append(pltpu.make_async_copy(hbm_in[i], bufs[i], in_sem.at[i]))
         loads[i].start()
-    if kind == FIRST:
-        again = pltpu.make_async_copy(hbm_in[2], tok_out, out_sem.at[5])
-        again.start()
     wk, toks = bufs[0], bufs[2:2 + nsrc]
     if kind == FIRST:
         wq = bufs[1]
@@ -152,6 +149,8 @@
         qn_ref, wqt = take(2)
         for load in loads:
             load.wait()
+        again = pltpu.make_async_copy(toks[0], tok_out, out_sem.at[5])
+        again.start()
         wqt[...] = wq[...].T
         wvt[...] = wk[:, wvt.shape[0]:].T
         qn_ref[...] = jnp.zeros_like(qn_ref)
@@ -312,7 +311,7 @@
     hbm = pl.BlockSpec(memory_space=pltpu.HBM)
     if kind == FIRST:
         big, small = [wk, wq, *toks], list(lists)
-        small_specs = [smem] * 3
+        small_specs = [smem] * 3 + [hbm]
         nqb = toks[0].shape[0] // BLOCK
     else:
         wvt, plan, qbd, *sums = state
@@ -403,7 +402,7 @@
     mate = send(tokens, [(i, i ^ 1) for i in everyone])
 
     wvt, plan, qbd, again, *sums = run_phase(
-        FIRST, [tokens], w_keyval, nbound, lists=(me, block_list, block_count), wq=w_query
+        FIRST, [tokens], w_keyval, nbound, lists=(me, block_list, block_count, rows), wq=w_query
     )
 
     hops = [(i, i + 1 if i % 2 else i - 1) for i in everyone]

time: 114 us -> 106 us (0.930)
  the two profiles are of different devices: /device:TPU:15 before, /device:TPU:5 now
where the time goes in v5:
time: 106 us; the launch traced here: 105 us
  Pallas kernels  68.7 us (65%)
  waiting for transfers between devices  14.1 us (13%)
  between operations  13.5 us (13%)
  starting transfers between devices  8.26 us (8%)
    pallas_call x3, Pallas kernels, run_phase(): pl.pallas_call(functools.partial(phase, kind, len(toks), nbound), out_sha...  66.3 us
    ppermute x4, waiting for transfers between devices, send(): return lax.ppermute(value, 'curve', pairs)  14.1 us
    ppermute x4, starting transfers between devices, send(): return lax.ppermute(value, 'curve', pairs)  8.26 us
    pallas_call x1, Pallas kernels, on_device(): pl.pallas_call(pick_rows, out_shape=jax.ShapeDtypeStruct((BCAP, width), j...  2.39 us
  transfers between devices with their start and end apart: 5, of which 2 were waited for; matrix products, arithmetic and copies ran while one was open for 0% of the time, Pallas kernels for 41%

profile of v5, /device:TPU:5, one launch (start us, length us, event | category | flops | bytes accessed | tf_op | source)
XLA Modules:
  0.0 104.6 jit_solution(3047097629513569656)
XLA Ops:
  6.5 0.0 all-gather.2.cloned.1.call-start
  6.5 4.2 %collective-permute-start.1 = (bf16[1024,512]{1,0:T(8,128)(2,1)}, bf16[1024,512]{1,0:T(8,128)(2,1)}, u32[]{:S(2)}, u32[]{:S(2)}) collective-permute-start(bf16[1024,512]{1,0:T(8,128)(2,1)} %refs_2_.1), channel_id=1, source_target_pairs={{0,2},{1,3},{2,4},{3,5},{4,6},{5,7},{8,10},{9,11},{10,12},{11,13},... | collective-permute-start | bytes 3145736 | tf_op jit(solution)/shard_map/ppermute | solution.py:377
  10.7 1.3 %collective-permute-start.2 = (bf16[1024,512]{1,0:T(8,128)(2,1)}, bf16[1024,512]{1,0:T(8,128)(2,1)}, u32[]{:S(2)}, u32[]{:S(2)}) collective-permute-start(bf16[1024,512]{1,0:T(8,128)(2,1)} %refs_2_.1), channel_id=1, source_target_pairs={{2,0},{3,1},{4,2},{5,3},{6,4},{7,5},{10,8},{11,9},{12,10},{13,11},... | collective-permute-start | bytes 3145736 | tf_op jit(solution)/shard_map/ppermute | solution.py:377
  12.0 0.3 collective-permute-start.3
  12.3 2.4 %pick_rows.1.refs_6_ = bf16[128,512]{1,0:T(8,128)(2,1)} custom-call(s32[1]{0:T(128)} %bitcast.me_ref.refs_3_, s32[1,512]{1,0:T(1,128)} %bitcast.2, bf16[1024,512]{1,0:T(8,128)(2,1)} %refs_2_.1), custom_call_target="tpu_custom_call" | custom-call | tf_op jit(solution)/shard_map/pick_rows/pallas_call | solution.py:390
  14.7 0.0 all-gather.2.cloned.1.call-update
  14.7 20.1 %attend_own.1 = (bf16[512,512]{1,0:T(8,128)(2,1)}, s32[8,128]{1,0:T(8,128)}, bf16[8,4,128,256]{3,2,1,0:T(8,128)(2,1)}, bf16[1024,512]{1,0:T(8,128)(2,1)}, f32[32...) custom-call(bf16[512,1024]{1,0:T(8,128)(2,1)} %refs_0_.5, bf16[512,512]{1,0:T(8,128)(2,1)} %refs_1_.1, ...), custom_call_target="tpu_custom_call" | custom-call | flops 5905580032 | bytes 8388608 | tf_op jit(solution)/shard_map/attend_own/pallas_call | solution.py:364
  34.8 2.5 %collective-permute-start = (bf16[1024,512]{1,0:T(8,128)(2,1)}, bf16[1024,512]{1,0:T(8,128)(2,1)}, u32[]{:S(2)}, u32[]{:S(2)}) collective-permute-start(bf16[1024,512]{1,0:T(8,128)(2,1)} %get-tuple-element.16), channel_id=1, source_target_pairs={{1,2},{2,1},{3,4},{4,3},{5,6},{6,5},{9,10},{10,9},{11,12},{12,11},... | collective-permute-start | bytes 3145736 | tf_op jit(solution)/shard_map/ppermute | solution.py:377
  37.3 0.0 collective-permute-done.1.refs_2_
  37.3 3.5 %collective-permute-done.2.refs_3_ = bf16[1024,512]{1,0:T(8,128)(2,1)} collective-permute-done((bf16[1024,512]{1,0:T(8,128)(2,1)}, bf16[1024,512]{1,0:T(8,128)(2,1)}, u32[]{:S(2)}, u32[]{:S(2)}) %collective-permute-start.2) | collective-permute-done | bytes 1048608 | tf_op jit(solution)/shard_map/ppermute | solution.py:377
  40.9 0.0 collective-permute-done.3.refs_4_
  40.9 20.3 %attend_middle.1 = (f32[32,128,128]{2,1,0:T(8,128)}, f32[33,1,256]{2,1,0:T(1,128)}, f32[32,1,256]{2,1,0:T(1,128)}) custom-call(bf16[512,1024]{1,0:T(8,128)(2,1)} %refs_0_.5, bf16[512,512]{1,0:T(8,128)(2,1)} %get-tuple-element.15.refs_1_, bf16[1024,512]{1,0:T(8,128)(2,1)} %collective-permute-done.1.refs_2_, bf16[1024,512]{1,0:T(8,128)(2,1)} %collective-permute-done.2.refs_3_, ...), custom_call_target="tpu_custom_call" | custom-call | flops 12348030976 | bytes 8388608 | tf_op jit(solution)/shard_map/attend_middle/pallas_call | solution.py:364
  61.1 10.6 %collective-permute-done.refs_2_ = bf16[1024,512]{1,0:T(8,128)(2,1)} collective-permute-done((bf16[1024,512]{1,0:T(8,128)(2,1)}, bf16[1024,512]{1,0:T(8,128)(2,1)}, u32[]{:S(2)}, u32[]{:S(2)}) %collective-permute-start) | collective-permute-done | bytes 1048608 | tf_op jit(solution)/shard_map/ppermute | solution.py:377
  71.7 0.0 all-gather.2.cloned.1.call-done.refs_7_
  71.7 26.0 %attend_last.1 = bf16[1024,512]{1,0:T(8,128)(2,1)} custom-call(bf16[512,1024]{1,0:T(8,128)(2,1)} %refs_0_.5, bf16[512,512]{1,0:T(8,128)(2,1)} %get-tuple-element.15.refs_1_, bf16[1024,512]{1,0:T(8,128)(2,1)} %collective-permute-done.refs_2_, bf16[8,4,128,256]{3,2,1,0:T(8,128)(2,1)} %get-tuple-element.17.refs_5_.refs_3_, ...), custom_call_target="tpu_custom_call" | custom-call | flops 13153337344 | bytes 8388608 | tf_op jit(solution)/shard_map/attend_last/pallas_call | solution.py:364
Async XLA Ops:
  6.5 65.2 %all-gather.2.cloned.1.call-start = ((), (), s32[]{:S(2)}) async-start(), calls=%async_computation | async-start | bytes 1179648 | tf_op jit(solution)/shard_map/all_gather | solution.py:398
  6.5 30.8 %collective-permute-start.1 = (bf16[1024,512]{1,0:T(8,128)(2,1)}, bf16[1024,512]{1,0:T(8,128)(2,1)}, u32[]{:S(2)}, u32[]{:S(2)}) collective-permute-start(bf16[1024,512]{1,0:T(8,128)(2,1)} %refs_2_.1), channel_id=1, source_target_pairs={{0,2},{1,3},{2,4},{3,5},{4,6},{5,7},{8,10},{9,11},{10,12},{11,13},... | collective-permute-start | bytes 3145736 | tf_op jit(solution)/shard_map/ppermute | solution.py:377
  10.7 30.1 %collective-permute-start.2 = (bf16[1024,512]{1,0:T(8,128)(2,1)}, bf16[1024,512]{1,0:T(8,128)(2,1)}, u32[]{:S(2)}, u32[]{:S(2)}) collective-permute-start(bf16[1024,512]{1,0:T(8,128)(2,1)} %refs_2_.1), channel_id=1, source_target_pairs={{2,0},{3,1},{4,2},{5,3},{6,4},{7,5},{10,8},{11,9},{12,10},{13,11},... | collective-permute-start | bytes 3145736 | tf_op jit(solution)/shard_map/ppermute | solution.py:377
  12.0 28.8 %collective-permute-start.3 = (bf16[1024,512]{1,0:T(8,128)(2,1)}, bf16[1024,512]{1,0:T(8,128)(2,1)}, u32[]{:S(2)}, u32[]{:S(2)}) collective-permute-start(bf16[1024,512]{1,0:T(8,128)(2,1)} %refs_2_.1), channel_id=1, source_target_pairs={{0,1},{1,0},{2,3},{3,2},{4,5},{5,4},{6,7},{7,6},{8,9},{9,8},{10,11... | collective-permute-start | bytes 3145736 | tf_op jit(solution)/shard_map/ppermute | solution.py:377
  34.8 36.9 %collective-permute-start = (bf16[1024,512]{1,0:T(8,128)(2,1)}, bf16[1024,512]{1,0:T(8,128)(2,1)}, u32[]{:S(2)}, u32[]{:S(2)}) collective-permute-start(bf16[1024,512]{1,0:T(8,128)(2,1)} %get-tuple-element.16), channel_id=1, source_target_pairs={{1,2},{2,1},{3,4},{4,3},{5,6},{6,5},{9,10},{10,9},{11,12},{12,11},... | collective-permute-start | bytes 3145736 | tf_op jit(solution)/shard_map/ppermute | solution.py:377
Sparse Core Ops, SparseCore 0:
  14.9 51.1 all-gather.1
